TPU v7x, 256 devices: a whole 4x4x8 slice. The times are simulated.
256 devices in a mesh: leaf: 64 (over z, y, core), rhs: 4 (over x).
Axes of the slice: x: 4, y: 4, z: 8, core: 2. Of those that a mesh axis runs over, the one named last changes fastest.
Arguments:
- points: bfloat16 [64, 524288], P('rhs', 'leaf'), may hold values from -6 to 6
- leaf_basis: bfloat16 [2048, 64, 256], P('leaf'), may hold values from -0.375 to 0.375
- local_transfer: bfloat16 [64, 31, 64, 128], P('leaf'), may hold values from -0.625 to 0.625
- top_transfer: bfloat16 [48, 64, 128], replicated, may hold values from -0.625 to 0.625
- leaf_coupling: bfloat16 [3, 2048, 64, 320], P(None, 'leaf'), may hold values from -0.3125 to 0.3125
- root_coupling: bfloat16 [3, 64, 64, 192], P(None, 'leaf'), may hold values from -0.4375 to 0.4375
- upper_coupling: bfloat16 [3, 48, 64, 192], replicated, may hold values from -0.4375 to 0.4375
- near_blocks: bfloat16 [3, 2048, 3, 256, 256], P(None, 'leaf', None, 'rhs'), may hold values from -0.21875 to 0.21875
- near_offset: int32 [2048, 3], P('leaf'), may hold values from -8 to 8, as said below
- far_offset: int32 [2048, 5], P('leaf'), may hold values from -8 to 8, as said below
Outputs:
- applied: bfloat16 [3, 64, 524288], P(None, 'rhs', 'leaf')
Inputs may be any that keep to these rules, and one draw needn't show every extreme that they name: `near_offset`: the first entry of each row is 0; the entries of a row are distinct and lie within 8 of 0. `far_offset`: entries are nonzero, distinct within a row, and differ from every entry of the same row of near_offset.
All inputs are finite; a program needn't handle non-finite values.
Results may differ from a plain program's by a relative error of at most 0.025.
Values may be sent and summed in bfloat16 or wider, within the bound.
No kernel may reach another device: no remote copies, remote signals or barrier semaphores. Data moves between devices by JAX's collectives and lax.ppermute only.
A program may use at most 192 MiB of HBM per device.

v0:
```python
import jax
import jax.numpy as jnp
from jax import lax
from jax.sharding import PartitionSpec as P

LEAF = 256
OPS = 3
W = 8
NEAR = 3
FAR = 5
TOPL = 3


def from_behind(block, axis, distance):
    devices = range(lax.axis_size(axis))
    route = [(i - distance, i) for i in devices if i - distance in devices]
    return lax.ppermute(block, axis, route)


def swapped(value, axis, distance):
    mask = 2**distance
    pairs = [(source, source ^ mask) for source in range(lax.axis_size(axis))]
    return lax.ppermute(value, axis, pairs)


def with_halo(cells, sides, width):
    for axis, dim in sides:
        count = lax.axis_size(axis)
        ends = count - 1
        head = lax.slice_in_dim(cells, 0, width, axis=dim)
        tail = lax.slice_in_dim(cells, cells.shape[dim] - width, cells.shape[dim], axis=dim)
        cells = jnp.concatenate(
            [
                lax.ppermute(tail, axis, [(i, (i + 1) % count) for i in range(ends)]),
                cells,
                lax.ppermute(head, axis, [((i + 1) % count, i) for i in range(ends)]),
            ],
            axis=dim,
        )
    return cells


def round_half(values):
    return values.astype(jnp.bfloat16)


def pair_up(level_coef, transfer):
    col_count, cluster_count, rank_size = level_coef.shape
    joined = level_coef.reshape(col_count, cluster_count // 2, 2 * rank_size)
    return round_half(
        jnp.einsum("cpk,prk->cpr", joined, transfer, preferred_element_type=jnp.float32)
    )


def pair_down(field, transfer):
    ops_count, col_count, cluster_count, rank_size = field.shape
    children = jnp.einsum(
        "ocpr,prk->ocpk", round_half(field), transfer, preferred_element_type=jnp.float32
    )
    return children.reshape(ops_count, col_count, 2 * cluster_count, rank_size)


def parity_sources(pieces, cluster):
    even_side = jnp.concatenate([pieces[-2], pieces[2], pieces[3]], axis=-1)
    odd_side = jnp.concatenate([pieces[-3], pieces[-2], pieces[2]], axis=-1)
    return jnp.where(cluster % 2 == 0, even_side, odd_side)


def couple_top(sources, coupling):
    return jnp.einsum("ck,ork->ocr", sources, coupling, preferred_element_type=jnp.float32)


def per_device(
    points,
    leaf_basis,
    local_transfer,
    top_transfer,
    leaf_coupling,
    root_coupling,
    upper_coupling,
    near_blocks,
    near_offset,
    far_offset,
):
    col_count, point_count = points.shape
    leaf_count = leaf_basis.shape[0]
    rank_size = leaf_basis.shape[1]
    groups = lax.axis_size("leaf")
    device = lax.axis_index("leaf")

    def top_rows(height):
        return groups - groups // 2 ** (height - 1)

    def coupling_at(height, cluster):
        if height == 0:
            return root_coupling[:, 0]
        return lax.dynamic_index_in_dim(
            upper_coupling, top_rows(height) + cluster, 1, keepdims=False
        )

    leaf_points = points.reshape(col_count, leaf_count, LEAF)
    leaf_coef = round_half(
        jnp.einsum("cti,tri->ctr", leaf_points, leaf_basis, preferred_element_type=jnp.float32)
    )
    depth_local = leaf_count.bit_length() - 1
    transfers = []
    current = leaf_coef
    offset = 0
    for height in range(depth_local):
        cluster_count = leaf_count >> height + 1
        transfer = local_transfer[0, offset : offset + cluster_count]
        transfers.append(transfer)
        current = pair_up(current, transfer)
        offset += cluster_count
    root_coef = current[:, 0]
    fields = []
    ancestor = root_coef
    for height in range(TOPL):
        cluster = device >> height
        pieces = {}
        for cousin in (-3, -2, 2, 3):
            distance = -cousin * 2**height
            pieces[cousin] = from_behind(ancestor, "leaf", distance)
        fields.append(couple_top(parity_sources(pieces, cluster), coupling_at(height, cluster)))
        if height + 1 < TOPL:
            partner = swapped(ancestor, "leaf", height)
            joined = jnp.where(
                cluster % 2 == 0,
                jnp.concatenate([ancestor, partner], axis=-1),
                jnp.concatenate([partner, ancestor], axis=-1),
            )
            parent_transfer = lax.dynamic_index_in_dim(
                top_transfer, top_rows(height + 1) + (cluster >> 1), 0, keepdims=False
            )
            ancestor = round_half(
                jnp.einsum("ck,rk->cr", joined, parent_transfer, preferred_element_type=jnp.float32)
            )
    running = fields[TOPL - 1]
    for height in range(TOPL - 1, 0, -1):
        cluster = device >> height
        transfer = lax.dynamic_index_in_dim(
            top_transfer, top_rows(height) + cluster, 0, keepdims=False
        )
        pushed = jnp.einsum(
            "ocr,rk->ock", round_half(running), transfer, preferred_element_type=jnp.float32
        )
        child_side = (device >> height - 1) % 2
        pushed_half = lax.dynamic_slice_in_dim(pushed, child_side * rank_size, rank_size, 2)
        running = fields[height - 1] + pushed_half
    field = running[:, :, None, :]
    for height in reversed(range(depth_local)):
        field = pair_down(field, transfers[height])
    leaf_range = jnp.arange(leaf_count, dtype=jnp.int32)[:, None]
    flat_coef = leaf_coef.reshape(col_count, leaf_count * rank_size)
    wide_coef = with_halo(flat_coef, (("leaf", 1),), W * rank_size).reshape(
        col_count, leaf_count + 2 * W, rank_size
    )
    far_index = W + leaf_range + far_offset
    sources = jnp.take(wide_coef, far_index.reshape(-1), axis=1).reshape(
        col_count, leaf_count, FAR * rank_size
    )
    coupled = jnp.einsum(
        "ctk,otrk->octr", sources, leaf_coupling, preferred_element_type=jnp.float32
    )
    leaf_field = round_half(field + coupled)
    far_part = jnp.einsum(
        "octr,tri->octi", leaf_field, leaf_basis, preferred_element_type=jnp.float32
    )
    wide_points = with_halo(points, (("leaf", 1),), W * LEAF).reshape(
        col_count, leaf_count + 2 * W, LEAF
    )
    near_index = W + leaf_range + near_offset
    all_wide = lax.all_gather(wide_points, "rhs", axis=0, tiled=True)
    all_columns = jnp.take(all_wide, near_index.reshape(-1), axis=1).reshape(
        all_wide.shape[0], leaf_count, NEAR, LEAF
    )
    row_terms = jnp.einsum(
        "ctkj,otkij->octi", all_columns, near_blocks, preferred_element_type=jnp.float32
    )
    near_part = lax.all_to_all(row_terms, "rhs", split_axis=1, concat_axis=3, tiled=True)
    result = (far_part + near_part).astype(jnp.bfloat16)
    return result.reshape(OPS, col_count, point_count)


def solution(mesh):
    placed = (
        P("rhs", "leaf"),
        P("leaf", None, None),
        P("leaf", None, None, None),
        P(),
        P(None, "leaf", None, None),
        P(None, "leaf", None, None),
        P(),
        P(None, "leaf", None, "rhs", None),
        P("leaf", None),
        P("leaf", None),
    )
    return jax.shard_map(
        per_device, mesh=mesh, in_specs=placed, out_specs=P(None, "rhs", "leaf"), check_vma=False
    )
```

profile of v0, /device:TPU:105, one launch (start us, length us, event | category | flops | bytes accessed | tf_op | source)
XLA Modules:
  0.0 167.0 jit_solution(4369492488095613762)
XLA Ops:
  6.6 1.0 fusion.193
  7.6 2.6 %collective-permute-start.17 = (bf16[16,2048]{1,0:T(8,128)(2,1)S(1)}, bf16[16,2048]{1,0:T(8,128)(2,1)S(1)}, u32[]{:S(2)}, u32[]{:S(2)}) collective-permute-start(bf16[16,2048]{1,0:T(8,128)(2,1)S(1)} %get-tuple-element.10), channel_id=1, source_target_pairs={{4,0},{8,4},{12,8},{16,12},{20,16},{24,20},{28,24},{32,28},{36,32}... | collective-permute-start | bytes 196616 | tf_op jit(solution)/shard_map/ppermute | solution.py:36
  10.2 3.1 %collective-permute-start.16 = (bf16[16,2048]{1,0:T(8,128)(2,1)S(1)}, bf16[16,2048]{1,0:T(8,128)(2,1)S(1)}, u32[]{:S(2)}, u32[]{:S(2)}) collective-permute-start(bf16[16,2048]{1,0:T(8,128)(2,1)S(1)} %get-tuple-element.9), channel_id=1, source_target_pairs={{0,4},{4,8},{8,12},{12,16},{16,20},{20,24},{24,28},{28,32},{32,36}... | collective-permute-start | bytes 196616 | tf_op jit(solution)/shard_map/ppermute | solution.py:34
  13.3 1.3 fusion.24
  14.7 0.1 reshape.144
  14.8 1.2 fusion.26
  16.2 1.1 fusion.28
  17.4 1.0 fusion.34
  18.5 0.1 fusion.39
  18.8 0.8 copy.202
  19.6 0.1 convolution_convert_fusion.12
  19.7 3.2 %collective-permute-start.2 = (bf16[16,64]{1,0:T(8,128)(2,1)S(1)}, bf16[16,64]{1,0:T(8,128)(2,1)S(1)}, u32[]{:S(2)}, u32[]{:S(2)}) collective-permute-start(bf16[16,64]{1,0:T(8,128)(2,1)S(1)} %convolution_convert_fusion.12), channel_id=1, source_target_pairs={{12,0},{16,4},{20,8},{24,12},{28,16},{32,20},{36,24},{40,28},{44,3... | collective-permute-start | bytes 6152 | tf_op jit(solution)/shard_map/ppermute | solution.py:17
  22.9 0.2 reshape.151
  23.2 0.1 reshape.155
  23.4 0.1 reshape.153
  23.5 0.6 fusion.194
  24.1 0.9 convolution_convert_fusion.11
  25.0 3.6 %collective-permute-start.9 = (bf16[16,64]{1,0:T(8,128)(2,1)S(1)}, bf16[16,64]{1,0:T(8,128)(2,1)S(1)}, u32[]{:S(2)}, u32[]{:S(2)}) collective-permute-start(bf16[16,64]{1,0:T(8,128)(2,1)S(1)} %convolution_convert_fusion.11), channel_id=1, source_target_pairs={{0,8},{4,12},{8,0},{12,4},{16,24},{20,28},{24,16},{28,20},{32,40},... | collective-permute-start | bytes 6152 | tf_op jit(solution)/shard_map/ppermute | solution.py:23
  28.6 1.0 collective-permute-done.9
  29.6 0.9 convolution_convert_fusion.10
  30.5 2.0 %collective-permute-start.12 = (bf16[16,64]{1,0:T(8,128)(2,1)S(1)}, bf16[16,64]{1,0:T(8,128)(2,1)S(1)}, u32[]{:S(2)}, u32[]{:S(2)}) collective-permute-start(bf16[16,64]{1,0:T(8,128)(2,1)S(1)} %convolution_convert_fusion.10), channel_id=1, source_target_pairs={{48,0},{52,4},{56,8},{60,12},{64,16},{68,20},{72,24},{76,28},{80,3... | collective-permute-start | bytes 6152 | tf_op jit(solution)/shard_map/ppermute | solution.py:17
  32.4 1.9 %collective-permute-start.11 = (bf16[16,64]{1,0:T(8,128)(2,1)S(1)}, bf16[16,64]{1,0:T(8,128)(2,1)S(1)}, u32[]{:S(2)}, u32[]{:S(2)}) collective-permute-start(bf16[16,64]{1,0:T(8,128)(2,1)S(1)} %convolution_convert_fusion.10), channel_id=1, source_target_pairs={{32,0},{36,4},{40,8},{44,12},{48,16},{52,20},{56,24},{60,28},{64,3... | collective-permute-start | bytes 6152 | tf_op jit(solution)/shard_map/ppermute | solution.py:17
  34.4 5.9 %collective-permute-start.10 = (bf16[16,64]{1,0:T(8,128)(2,1)S(1)}, bf16[16,64]{1,0:T(8,128)(2,1)S(1)}, u32[]{:S(2)}, u32[]{:S(2)}) collective-permute-start(bf16[16,64]{1,0:T(8,128)(2,1)S(1)} %convolution_convert_fusion.10), channel_id=1, source_target_pairs={{0,32},{4,36},{8,40},{12,44},{16,48},{20,52},{24,56},{28,60},{32,6... | collective-permute-start | bytes 6152 | tf_op jit(solution)/shard_map/ppermute | solution.py:17
  40.3 5.8 %collective-permute-start.13 = (bf16[16,64]{1,0:T(8,128)(2,1)S(1)}, bf16[16,64]{1,0:T(8,128)(2,1)S(1)}, u32[]{:S(2)}, u32[]{:S(2)}) collective-permute-start(bf16[16,64]{1,0:T(8,128)(2,1)S(1)} %convolution_convert_fusion.10), channel_id=1, source_target_pairs={{0,48},{4,52},{8,56},{12,60},{16,64},{20,68},{24,72},{28,76},{32,8... | collective-permute-start | bytes 6152 | tf_op jit(solution)/shard_map/ppermute | solution.py:17
  46.1 0.1 copy.138
  46.2 0.1 copy.130
  46.4 0.1 broadcast_in_dim.27
  46.6 2.8 %collective-permute-start.7 = (bf16[16,64]{1,0:T(8,128)(2,1)S(1)}, bf16[16,64]{1,0:T(8,128)(2,1)S(1)}, u32[]{:S(2)}, u32[]{:S(2)}) collective-permute-start(bf16[16,64]{1,0:T(8,128)(2,1)S(1)} %convolution_convert_fusion.11), channel_id=1, source_target_pairs={{24,0},{28,4},{32,8},{36,12},{40,16},{44,20},{48,24},{52,28},{56,3... | collective-permute-start | bytes 6152 | tf_op jit(solution)/shard_map/ppermute | solution.py:17
  49.4 2.6 %collective-permute-start.6 = (bf16[16,64]{1,0:T(8,128)(2,1)S(1)}, bf16[16,64]{1,0:T(8,128)(2,1)S(1)}, u32[]{:S(2)}, u32[]{:S(2)}) collective-permute-start(bf16[16,64]{1,0:T(8,128)(2,1)S(1)} %convolution_convert_fusion.11), channel_id=1, source_target_pairs={{16,0},{20,4},{24,8},{28,12},{32,16},{36,20},{40,24},{44,28},{48,3... | collective-permute-start | bytes 6152 | tf_op jit(solution)/shard_map/ppermute | solution.py:17
  52.0 4.2 %collective-permute-start.5 = (bf16[16,64]{1,0:T(8,128)(2,1)S(1)}, bf16[16,64]{1,0:T(8,128)(2,1)S(1)}, u32[]{:S(2)}, u32[]{:S(2)}) collective-permute-start(bf16[16,64]{1,0:T(8,128)(2,1)S(1)} %convolution_convert_fusion.11), channel_id=1, source_target_pairs={{0,16},{4,20},{8,24},{12,28},{16,32},{20,36},{24,40},{28,44},{32,4... | collective-permute-start | bytes 6152 | tf_op jit(solution)/shard_map/ppermute | solution.py:17
  56.2 4.6 %collective-permute-start.8 = (bf16[16,64]{1,0:T(8,128)(2,1)S(1)}, bf16[16,64]{1,0:T(8,128)(2,1)S(1)}, u32[]{:S(2)}, u32[]{:S(2)}) collective-permute-start(bf16[16,64]{1,0:T(8,128)(2,1)S(1)} %convolution_convert_fusion.11), channel_id=1, source_target_pairs={{0,24},{4,28},{8,32},{12,36},{16,40},{20,44},{24,48},{28,52},{32,5... | collective-permute-start | bytes 6152 | tf_op jit(solution)/shard_map/ppermute | solution.py:17
  60.8 1.2 fusion.36
  62.0 4.6 %collective-permute-start.1 = (bf16[16,64]{1,0:T(8,128)(2,1)S(1)}, bf16[16,64]{1,0:T(8,128)(2,1)S(1)}, u32[]{:S(2)}, u32[]{:S(2)}) collective-permute-start(bf16[16,64]{1,0:T(8,128)(2,1)S(1)} %convolution_convert_fusion.12), channel_id=1, source_target_pairs={{8,0},{12,4},{16,8},{20,12},{24,16},{28,20},{32,24},{36,28},{40,32... | collective-permute-start | bytes 6152 | tf_op jit(solution)/shard_map/ppermute | solution.py:17
  66.6 1.9 %collective-permute-start = (bf16[16,64]{1,0:T(8,128)(2,1)S(1)}, bf16[16,64]{1,0:T(8,128)(2,1)S(1)}, u32[]{:S(2)}, u32[]{:S(2)}) collective-permute-start(bf16[16,64]{1,0:T(8,128)(2,1)S(1)} %convolution_convert_fusion.12), channel_id=1, source_target_pairs={{0,8},{4,12},{8,16},{12,20},{16,24},{20,28},{24,32},{28,36},{32,40... | collective-permute-start | bytes 6152 | tf_op jit(solution)/shard_map/ppermute | solution.py:17
  68.6 10.6 %collective-permute-start.3 = (bf16[16,64]{1,0:T(8,128)(2,1)S(1)}, bf16[16,64]{1,0:T(8,128)(2,1)S(1)}, u32[]{:S(2)}, u32[]{:S(2)}) collective-permute-start(bf16[16,64]{1,0:T(8,128)(2,1)S(1)} %convolution_convert_fusion.12), channel_id=1, source_target_pairs={{0,12},{4,16},{8,20},{12,24},{16,28},{20,32},{24,36},{28,40},{32,4... | collective-permute-start | bytes 6152 | tf_op jit(solution)/shard_map/ppermute | solution.py:17
  79.2 1.9 %collective-permute-start.15 = (bf16[16,512]{1,0:T(8,128)(2,1)}, bf16[16,512]{1,0:T(8,128)(2,1)S(1)}, u32[]{:S(2)}, u32[]{:S(2)}) collective-permute-start(bf16[16,512]{1,0:T(8,128)(2,1)} %get-tuple-element.12), channel_id=1, source_target_pairs={{4,0},{8,4},{12,8},{16,12},{20,16},{24,20},{28,24},{32,28},{36,32}... | collective-permute-start | bytes 49160 | tf_op jit(solution)/shard_map/ppermute | solution.py:36
  81.1 1.2 fusion.38
  82.4 3.6 %collective-permute-start.14 = (bf16[16,512]{1,0:T(8,128)(2,1)S(1)}, bf16[16,512]{1,0:T(8,128)(2,1)S(1)}, u32[]{:S(2)}, u32[]{:S(2)}) collective-permute-start(bf16[16,512]{1,0:T(8,128)(2,1)S(1)} %get-tuple-element.11), channel_id=1, source_target_pairs={{0,4},{4,8},{8,12},{12,16},{16,20},{20,24},{24,28},{28,32},{32,36}... | collective-permute-start | bytes 49160 | tf_op jit(solution)/shard_map/ppermute | solution.py:34
  86.1 0.3 fusion.37
  86.5 0.1 fusion.29
  86.8 3.9 %gather_fusion.1 = bf16[96,64,256]{2,1,0:T(8,128)(2,1)} fusion(bf16[64,48,256]{2,0,1:T(8,128)(2,1)} %all-gather.2.cloned.1.call-done, s32[1024]{0:T(1024)S(1)} %pad_clamp_fusion), kind=kCustom, calls=%fused_computation.1 | custom fusion | bytes 6291840 | tf_op jit(solution)/shard_map/jit(_take)/gather | solution.py:174
  90.7 8.3 %fusion.7 = f32[3,64,32,64]{3,1,0,2:T(8,128)S(1)} fusion(bf16[3,32,3,64,256]{4,3,2,1,0:T(8,128)(2,1)} %param.17, bf16[64,32,3,256]{3,0,2,1:T(8,128)(2,1)} %bitcast.195, pred[32,3]{1,0:T(8,128)(4,1)S(1)} %copy.138), kind=kOutput, calls=%fused_computation.10 | convolution fusion | flops 605552640 | bytes 14155872 | tf_op jit(solution)/shard_map/ctkj,otkij->octi/dot_general | solution.py:177
  99.0 3.5 %copy.203 = f32[3,64,32,64]{3,2,0,1:T(8,128)} copy(f32[3,64,32,64]{3,1,0,2:T(8,128)S(1)} %fusion.7) | data formatting | bytes 3145728 | tf_op jit(solution)/shard_map/ctkj,otkij->octi/transpose | solution.py:177
  102.5 4.8 %reshape.187 = f32[4,1,98304]{2,1,0:T(1,128)} reshape(f32[64,3,32,64]{3,2,1,0:T(8,128)} %bitcast.192) | data formatting | bytes 3145728
  107.3 4.0 %all-to-all-start = ((f32[4,1,98304]{2,1,0:T(1,128)}), f32[4,1,98304]{2,1,0:T(1,128)S(1)}, u32[]{:S(2)}, u32[]{:S(2)}) async-start(f32[4,1,98304]{2,1,0:T(1,128)} %reshape.187), calls=%async_computation | async-start | bytes 3145728 | tf_op jit(solution)/shard_map/all_to_all | solution.py:180
  111.3 0.2 fusion.27
  111.6 0.2 fusion.25
  111.8 0.1 convert_element_type.133
  112.0 0.2 convolution_bitcast_fusion
  112.2 0.1 copy.129
  112.3 1.1 reshape.150
  113.4 0.2 reshape.152
  113.7 0.7 gather_fusion
  114.4 1.0 copy.134
  115.4 1.6 gather.13
  117.0 0.8 select_bitcast_fusion
  117.8 14.0 %all-to-all-done = f32[4,1,98304]{2,1,0:T(1,128)S(1)} async-done(((f32[4,1,98304]{2,1,0:T(1,128)}), f32[4,1,98304]{2,1,0:T(1,128)S(1)}, u32[]{:S(2)}, u32[]{:S(2)}) %all-to-all-start) | async-done | bytes 1572896 | tf_op jit(solution)/shard_map/all_to_all | solution.py:180
  131.8 0.5 broadcast.83
  132.4 6.4 %reduce = f32[4,98304]{1,0:T(4,128)} reduce(f32[4,1,98304]{2,1,0:T(1,128)S(1)} %all-to-all-done, f32[]{:T(128)} %broadcast.83), dimensions={1}, to_apply=%all_to_all.13.reduce_sub_computation | reduce | bytes 3145732 | tf_op jit(solution)/shard_map/all_to_all | solution.py:180
  138.7 4.5 %reshape.188 = f32[64,3,32,64]{3,2,1,0:T(8,128)} reshape(f32[4,98304]{1,0:T(4,128)} %reduce) | data formatting | bytes 3145728
  143.3 5.6 %copy.201 = f32[3,4,16,32,64]{4,1,2,0,3:T(4,128)} copy(f32[3,4,16,32,64]{4,3,0,2,1:T(8,128)} %bitcast.193) | data formatting | bytes 3145728 | tf_op jit(solution)/shard_map/all_to_all | solution.py:180
  148.9 3.3 %all_to_all.16 = f32[3,16,32,256]{3,1,0,2:T(8,128)S(1)} reshape(f32[3,16,32,4,64]{4,3,1,0,2:T(4,128)} %bitcast.194) | data formatting | bytes 3145728 | tf_op jit(solution)/shard_map/all_to_all | solution.py:180
  152.2 5.9 %fusion.14 = bf16[32,3,2,8,256]{4,3,2,1,0:T(8,128)(2,1)} fusion(f32[3,16,32,256]{3,1,0,2:T(8,128)S(1)} %all_to_all.16, bf16[32,64,256]{2,1,0:T(8,128)(2,1)S(1)} %copy-done, bf16[3,32,64,320]{3,2,1,0:T(8,128)(2,1)} %param.14, f32[3,16,32,64]{3,2,1,0:T(8,128)S(1)} %copy-done.1, bf16[16,32,320,1]{2,1,0,3:T(8,128)(2,1)} %select_bitcast_fusion), kind=kOutput, calls=%fused_computation.14 | convolution fusion | flops 114229248 | bytes 8060928 | tf_op jit(solution)/shard_map/octr,tri->octi/dot_general | solution.py:166
  158.1 2.1 %copy.157 = bf16[32,3,2,8,256]{4,3,0,2,1:T(8,128)(2,1)} copy(bf16[32,3,2,8,256]{4,3,2,1,0:T(8,128)(2,1)} %fusion.14) | data formatting | bytes 1572864 | tf_op jit(solution)/shard_map/reshape | solution.py:182
  (63 shorter events, 1.5 us)
Async XLA Ops:
  6.5 6.8 %copy-start = (bf16[32,64,256]{2,1,0:T(8,128)(2,1)S(1)}, bf16[32,64,256]{2,1,0:T(8,128)(2,1)}, u32[]{:S(2)}) copy-start(bf16[32,64,256]{2,1,0:T(8,128)(2,1)} %param.11) | copy-start | bytes 3145732
  6.5 12.2 %copy-start.3 = (bf16[16,8192]{1,0:T(8,128)(2,1)S(1)}, bf16[16,8192]{1,0:T(8,128)(2,1)}, u32[]{:S(2)}) copy-start(bf16[16,8192]{1,0:T(8,128)(2,1)} %param.10) | copy-start | bytes 786436
  6.5 11.9 %copy-start.2 = (bf16[1,31,64,128]{3,2,1,0:T(8,128)(2,1)S(1)}, bf16[1,31,64,128]{3,2,1,0:T(8,128)(2,1)}, u32[]{:S(2)}) copy-start(bf16[1,31,64,128]{3,2,1,0:T(8,128)(2,1)} %param.12) | copy-start | bytes 1523716
  6.5 16.5 %copy-start.6 = (s32[32,3]{0,1:T(4,128)S(1)}, s32[32,3]{0,1:T(4,128)}, u32[]{:S(2)}) copy-start(s32[32,3]{0,1:T(4,128)} %param.18) | copy-start | bytes 1156
  6.5 16.7 %copy-start.5 = (s32[32,5]{0,1:T(8,128)S(1)}, s32[32,5]{0,1:T(8,128)}, u32[]{:S(2)}) copy-start(s32[32,5]{0,1:T(8,128)} %param.19) | copy-start | bytes 1924
  6.5 79.5 %copy-start.4 = (bf16[3,1,64,192]{3,2,1,0:T(8,128)(2,1)S(1)}, bf16[3,1,64,192]{3,2,1,0:T(8,128)(2,1)}, u32[]{:S(2)}) copy-start(bf16[3,1,64,192]{3,2,1,0:T(8,128)(2,1)} %param.15) | copy-start | bytes 221188
  6.6 80.2 %all-gather.2.cloned.1.call-start = ((), (), s32[]{:S(2)}) async-start(), calls=%async_computation.1 | async-start | bytes 1966080 | tf_op jit(solution)/shard_map/all_gather | solution.py:173
  7.6 11.1 %collective-permute-start.17 = (bf16[16,2048]{1,0:T(8,128)(2,1)S(1)}, bf16[16,2048]{1,0:T(8,128)(2,1)S(1)}, u32[]{:S(2)}, u32[]{:S(2)}) collective-permute-start(bf16[16,2048]{1,0:T(8,128)(2,1)S(1)} %get-tuple-element.10), channel_id=1, source_target_pairs={{4,0},{8,4},{12,8},{16,12},{20,16},{24,20},{28,24},{32,28},{36,32}... | collective-permute-start | bytes 196616 | tf_op jit(solution)/shard_map/ppermute | solution.py:36
  10.2 8.5 %collective-permute-start.16 = (bf16[16,2048]{1,0:T(8,128)(2,1)S(1)}, bf16[16,2048]{1,0:T(8,128)(2,1)S(1)}, u32[]{:S(2)}, u32[]{:S(2)}) collective-permute-start(bf16[16,2048]{1,0:T(8,128)(2,1)S(1)} %get-tuple-element.9), channel_id=1, source_target_pairs={{0,4},{4,8},{8,12},{12,16},{16,20},{20,24},{24,28},{28,32},{32,36}... | collective-permute-start | bytes 196616 | tf_op jit(solution)/shard_map/ppermute | solution.py:34
  19.7 4.4 %collective-permute-start.4 = (bf16[16,64]{1,0:T(8,128)(2,1)S(1)}, bf16[16,64]{1,0:T(8,128)(2,1)S(1)}, u32[]{:S(2)}, u32[]{:S(2)}) collective-permute-start(bf16[16,64]{1,0:T(8,128)(2,1)S(1)} %convolution_convert_fusion.12), channel_id=1, source_target_pairs={{0,4},{4,0},{8,12},{12,8},{16,20},{20,16},{24,28},{28,24},{32,36},... | collective-permute-start | bytes 6152 | tf_op jit(solution)/shard_map/ppermute | solution.py:23
  19.7 62.7 %collective-permute-start.2 = (bf16[16,64]{1,0:T(8,128)(2,1)S(1)}, bf16[16,64]{1,0:T(8,128)(2,1)S(1)}, u32[]{:S(2)}, u32[]{:S(2)}) collective-permute-start(bf16[16,64]{1,0:T(8,128)(2,1)S(1)} %convolution_convert_fusion.12), channel_id=1, source_target_pairs={{12,0},{16,4},{20,8},{24,12},{28,16},{32,20},{36,24},{40,28},{44,3... | collective-permute-start | bytes 6152 | tf_op jit(solution)/shard_map/ppermute | solution.py:17
  25.0 4.6 %collective-permute-start.9 = (bf16[16,64]{1,0:T(8,128)(2,1)S(1)}, bf16[16,64]{1,0:T(8,128)(2,1)S(1)}, u32[]{:S(2)}, u32[]{:S(2)}) collective-permute-start(bf16[16,64]{1,0:T(8,128)(2,1)S(1)} %convolution_convert_fusion.11), channel_id=1, source_target_pairs={{0,8},{4,12},{8,0},{12,4},{16,24},{20,28},{24,16},{28,20},{32,40},... | collective-permute-start | bytes 6152 | tf_op jit(solution)/shard_map/ppermute | solution.py:23
  30.5 16.1 %collective-permute-start.12 = (bf16[16,64]{1,0:T(8,128)(2,1)S(1)}, bf16[16,64]{1,0:T(8,128)(2,1)S(1)}, u32[]{:S(2)}, u32[]{:S(2)}) collective-permute-start(bf16[16,64]{1,0:T(8,128)(2,1)S(1)} %convolution_convert_fusion.10), channel_id=1, source_target_pairs={{48,0},{52,4},{56,8},{60,12},{64,16},{68,20},{72,24},{76,28},{80,3... | collective-permute-start | bytes 6152 | tf_op jit(solution)/shard_map/ppermute | solution.py:17
  32.4 16.9 %collective-permute-start.11 = (bf16[16,64]{1,0:T(8,128)(2,1)S(1)}, bf16[16,64]{1,0:T(8,128)(2,1)S(1)}, u32[]{:S(2)}, u32[]{:S(2)}) collective-permute-start(bf16[16,64]{1,0:T(8,128)(2,1)S(1)} %convolution_convert_fusion.10), channel_id=1, source_target_pairs={{32,0},{36,4},{40,8},{44,12},{48,16},{52,20},{56,24},{60,28},{64,3... | collective-permute-start | bytes 6152 | tf_op jit(solution)/shard_map/ppermute | solution.py:17
  34.4 17.6 %collective-permute-start.10 = (bf16[16,64]{1,0:T(8,128)(2,1)S(1)}, bf16[16,64]{1,0:T(8,128)(2,1)S(1)}, u32[]{:S(2)}, u32[]{:S(2)}) collective-permute-start(bf16[16,64]{1,0:T(8,128)(2,1)S(1)} %convolution_convert_fusion.10), channel_id=1, source_target_pairs={{0,32},{4,36},{8,40},{12,44},{16,48},{20,52},{24,56},{28,60},{32,6... | collective-permute-start | bytes 6152 | tf_op jit(solution)/shard_map/ppermute | solution.py:17
  40.3 15.8 %collective-permute-start.13 = (bf16[16,64]{1,0:T(8,128)(2,1)S(1)}, bf16[16,64]{1,0:T(8,128)(2,1)S(1)}, u32[]{:S(2)}, u32[]{:S(2)}) collective-permute-start(bf16[16,64]{1,0:T(8,128)(2,1)S(1)} %convolution_convert_fusion.10), channel_id=1, source_target_pairs={{0,48},{4,52},{8,56},{12,60},{16,64},{20,68},{24,72},{28,76},{32,8... | collective-permute-start | bytes 6152 | tf_op jit(solution)/shard_map/ppermute | solution.py:17
  46.6 15.5 %collective-permute-start.7 = (bf16[16,64]{1,0:T(8,128)(2,1)S(1)}, bf16[16,64]{1,0:T(8,128)(2,1)S(1)}, u32[]{:S(2)}, u32[]{:S(2)}) collective-permute-start(bf16[16,64]{1,0:T(8,128)(2,1)S(1)} %convolution_convert_fusion.11), channel_id=1, source_target_pairs={{24,0},{28,4},{32,8},{36,12},{40,16},{44,20},{48,24},{52,28},{56,3... | collective-permute-start | bytes 6152 | tf_op jit(solution)/shard_map/ppermute | solution.py:17
  49.4 17.3 %collective-permute-start.6 = (bf16[16,64]{1,0:T(8,128)(2,1)S(1)}, bf16[16,64]{1,0:T(8,128)(2,1)S(1)}, u32[]{:S(2)}, u32[]{:S(2)}) collective-permute-start(bf16[16,64]{1,0:T(8,128)(2,1)S(1)} %convolution_convert_fusion.11), channel_id=1, source_target_pairs={{16,0},{20,4},{24,8},{28,12},{32,16},{36,20},{40,24},{44,28},{48,3... | collective-permute-start | bytes 6152 | tf_op jit(solution)/shard_map/ppermute | solution.py:17
  52.0 16.6 %collective-permute-start.5 = (bf16[16,64]{1,0:T(8,128)(2,1)S(1)}, bf16[16,64]{1,0:T(8,128)(2,1)S(1)}, u32[]{:S(2)}, u32[]{:S(2)}) collective-permute-start(bf16[16,64]{1,0:T(8,128)(2,1)S(1)} %convolution_convert_fusion.11), channel_id=1, source_target_pairs={{0,16},{4,20},{8,24},{12,28},{16,32},{20,36},{24,40},{28,44},{32,4... | collective-permute-start | bytes 6152 | tf_op jit(solution)/shard_map/ppermute | solution.py:17
  56.2 23.0 %collective-permute-start.8 = (bf16[16,64]{1,0:T(8,128)(2,1)S(1)}, bf16[16,64]{1,0:T(8,128)(2,1)S(1)}, u32[]{:S(2)}, u32[]{:S(2)}) collective-permute-start(bf16[16,64]{1,0:T(8,128)(2,1)S(1)} %convolution_convert_fusion.11), channel_id=1, source_target_pairs={{0,24},{4,28},{8,32},{12,36},{16,40},{20,44},{24,48},{28,52},{32,5... | collective-permute-start | bytes 6152 | tf_op jit(solution)/shard_map/ppermute | solution.py:17
  62.0 24.0 %collective-permute-start.1 = (bf16[16,64]{1,0:T(8,128)(2,1)S(1)}, bf16[16,64]{1,0:T(8,128)(2,1)S(1)}, u32[]{:S(2)}, u32[]{:S(2)}) collective-permute-start(bf16[16,64]{1,0:T(8,128)(2,1)S(1)} %convolution_convert_fusion.12), channel_id=1, source_target_pairs={{8,0},{12,4},{16,8},{20,12},{24,16},{28,20},{32,24},{36,28},{40,32... | collective-permute-start | bytes 6152 | tf_op jit(solution)/shard_map/ppermute | solution.py:17
  66.6 19.4 %collective-permute-start = (bf16[16,64]{1,0:T(8,128)(2,1)S(1)}, bf16[16,64]{1,0:T(8,128)(2,1)S(1)}, u32[]{:S(2)}, u32[]{:S(2)}) collective-permute-start(bf16[16,64]{1,0:T(8,128)(2,1)S(1)} %convolution_convert_fusion.12), channel_id=1, source_target_pairs={{0,8},{4,12},{8,16},{12,20},{16,24},{20,28},{24,32},{28,36},{32,40... | collective-permute-start | bytes 6152 | tf_op jit(solution)/shard_map/ppermute | solution.py:17
  68.6 17.5 %collective-permute-start.3 = (bf16[16,64]{1,0:T(8,128)(2,1)S(1)}, bf16[16,64]{1,0:T(8,128)(2,1)S(1)}, u32[]{:S(2)}, u32[]{:S(2)}) collective-permute-start(bf16[16,64]{1,0:T(8,128)(2,1)S(1)} %convolution_convert_fusion.12), channel_id=1, source_target_pairs={{0,12},{4,16},{8,20},{12,24},{16,28},{20,32},{24,36},{28,40},{32,4... | collective-permute-start | bytes 6152 | tf_op jit(solution)/shard_map/ppermute | solution.py:17
  79.2 34.2 %collective-permute-start.15 = (bf16[16,512]{1,0:T(8,128)(2,1)}, bf16[16,512]{1,0:T(8,128)(2,1)S(1)}, u32[]{:S(2)}, u32[]{:S(2)}) collective-permute-start(bf16[16,512]{1,0:T(8,128)(2,1)} %get-tuple-element.12), channel_id=1, source_target_pairs={{4,0},{8,4},{12,8},{16,12},{20,16},{24,20},{28,24},{32,28},{36,32}... | collective-permute-start | bytes 49160 | tf_op jit(solution)/shard_map/ppermute | solution.py:36
  82.4 31.1 %collective-permute-start.14 = (bf16[16,512]{1,0:T(8,128)(2,1)S(1)}, bf16[16,512]{1,0:T(8,128)(2,1)S(1)}, u32[]{:S(2)}, u32[]{:S(2)}) collective-permute-start(bf16[16,512]{1,0:T(8,128)(2,1)S(1)} %get-tuple-element.11), channel_id=1, source_target_pairs={{0,4},{4,8},{8,12},{12,16},{16,20},{20,24},{24,28},{28,32},{32,36}... | collective-permute-start | bytes 49160 | tf_op jit(solution)/shard_map/ppermute | solution.py:34
  107.3 24.5 %all-to-all-start = ((f32[4,1,98304]{2,1,0:T(1,128)}), f32[4,1,98304]{2,1,0:T(1,128)S(1)}, u32[]{:S(2)}, u32[]{:S(2)}) async-start(f32[4,1,98304]{2,1,0:T(1,128)} %reshape.187), calls=%async_computation | async-start | bytes 3145728 | tf_op jit(solution)/shard_map/all_to_all | solution.py:180
  148.9 3.3 %copy-start.1 = (f32[3,16,32,64]{3,2,1,0:T(8,128)S(1)}, f32[3,16,32,64]{3,2,1,0:T(8,128)}, u32[]{:S(2)}) copy-start(f32[3,16,32,64]{3,2,1,0:T(8,128)} %reshape.150) | copy-start | bytes 1179652
Sparse Core Ops, SparseCore 0:
  19.7 32.1 all-gather.1
where the time goes:
time: 168 us; the launch traced here: 167 us
  starting transfers between devices  68.9 us (41%)
  local copies, waits for them, and re-layouts  37.6 us (22%)
  matrix products  24.2 us (14%)
  waiting for transfers between devices  15.1 us (9%)
  between operations  14 us (8%)
  other arithmetic  7.26 us (4%)
    ppermute x12, starting transfers between devices, from_behind(): return lax.ppermute(block, axis, route)  50 us
    all_to_all x1, waiting for transfers between devices, per_device(): lax.all_to_all(row_terms, 'rhs', split_axis=1, concat_axis=3, tiled=True)  14 us
    all_to_all x3, local copies, waits for them, and re-layouts, per_device(): lax.all_to_all(row_terms, 'rhs', split_axis=1, concat_axis=3, tiled=True)  9.47 us
    unnamed x16, local copies, waits for them, and re-layouts  9.37 us
    dot_general x1, matrix products, per_device(): jnp.einsum('ctkj,otkij->octi', all_columns, near_blocks, preferred_elemen...  8.31 us
    ppermute x2, starting transfers between devices, with_halo(): lax.ppermute(tail, axis, [(i, (i + 1) % count) for i in range(ends)])  6.74 us
    all_to_all x1, other arithmetic, per_device(): lax.all_to_all(row_terms, 'rhs', split_axis=1, concat_axis=3, tiled=True)  6.38 us
    dot_general x1, matrix products, per_device(): jnp.einsum('octr,tri->octi', leaf_field, leaf_basis, preferred_element_ty...  5.88 us
  transfers between devices with their start and end apart: 20, of which 2 were waited for; matrix products, arithmetic and copies ran while one was open for 23% of the time, Pallas kernels for 0%

commit v1 on v0

v1 whole, which is shorter than its diff:
```python
import functools

import jax
import jax.numpy as jnp
from jax import lax
from jax.experimental import pallas as pl
from jax.experimental.pallas import tpu as pltpu
from jax.sharding import PartitionSpec as P

LEAF = 256
RANK = 64
OPS = 3
W = 8
NEAR = 3
FAR = 5
COLS = 16
LEAVES = 32
ROOTS = 64
SIDES = 4
PAIRS = LEAVES // 2

NT = (((1,), (1,)), ((), ()))
NN = (((1,), (0,)), ((), ()))
F32 = jnp.float32
BF16 = jnp.bfloat16

VMEM = pl.BlockSpec(memory_space=pltpu.VMEM)
SMEM = pl.BlockSpec(memory_space=pltpu.SMEM)
ANY = pl.BlockSpec(memory_space=pl.ANY)


def dot_nt(a, b):
    return lax.dot_general(a, b, NT, preferred_element_type=F32)


def dot_nn(a, b):
    return lax.dot_general(a, b, NN, preferred_element_type=F32)


def params(mib):
    return pltpu.CompilerParams(vmem_limit_bytes=mib * 2**20)


def cost(flops, bytes_accessed):
    return pl.CostEstimate(flops=flops, bytes_accessed=bytes_accessed, transcendentals=0)


def up_kernel(points_ref, basis_ref, transfer_ref, pairs_ref, root_ref):
    level = []
    for pair in range(PAIRS):
        halves = [
            dot_nt(points_ref[:, t * LEAF : (t + 1) * LEAF], basis_ref[t])
            for t in (2 * pair, 2 * pair + 1)
        ]
        joined = jnp.concatenate(halves, axis=1).astype(BF16)
        pairs_ref[pair] = joined
        level.append(joined)
    first = 0
    while True:
        parents = [dot_nt(joined, transfer_ref[first + i]) for i, joined in enumerate(level)]
        first += len(level)
        if len(parents) == 1:
            break
        level = [
            jnp.concatenate(parents[i : i + 2], axis=1).astype(BF16)
            for i in range(0, len(parents), 2)
        ]
    root = parents[0].astype(BF16)
    for slot in range(ROOTS):
        root_ref[slot * COLS : (slot + 1) * COLS] = root


def upsweep(points, leaf_basis, transfer):
    return pl.pallas_call(
        up_kernel,
        in_specs=[VMEM] * 3,
        out_specs=[VMEM] * 2,
        out_shape=[
            jax.ShapeDtypeStruct((PAIRS, COLS, 2 * RANK), BF16),
            jax.ShapeDtypeStruct((ROOTS * COLS, RANK), BF16),
        ],
        compiler_params=params(8),
        cost_estimate=cost(2**25, 2**21),
        name="upsweep",
    )(points, leaf_basis, transfer)


def near_leaf(sources, blocks_ref, t):
    wide = jnp.concatenate(sources, axis=1)
    block = jnp.concatenate(
        [blocks_ref[:, t, k].reshape(OPS * RANK, LEAF) for k in range(NEAR)], axis=1
    )
    return dot_nt(wide, block)


def store_pair(out_refs, slot, results):
    both = jnp.concatenate(results, axis=1).astype(BF16)
    for side, out_ref in enumerate(out_refs):
        out_ref[slot * COLS : (slot + 1) * COLS] = both[side * COLS : (side + 1) * COLS]


def inner_kernel(offset_ref, p0, p1, p2, p3, blocks_ref, *out_refs):
    for pair in range(W // 2, PAIRS - W // 2):
        results = []
        for t in (2 * pair, 2 * pair + 1):
            sources = []
            for k in range(NEAR):
                start = pl.multiple_of((t + offset_ref[t, k]) * LEAF, LEAF)
                sources.append(
                    jnp.concatenate([p[:, pl.ds(start, LEAF)] for p in (p0, p1, p2, p3)], axis=0)
                )
            results.append(near_leaf(sources, blocks_ref, t))
        store_pair(out_refs, pair - W // 2, results)


def outer_kernel(offset_ref, p0, p1, p2, p3, left_ref, right_ref, blocks_ref, *refs):
    out_refs, window = refs[:SIDES], refs[SIDES]
    span = W * LEAF
    for side, part in enumerate((0, 1)):
        base = part * (LEAVES - 2 * W) * LEAF
        halo_at, own_at = (0, span) if part == 0 else (2 * span, 0)
        halo_ref = left_ref if part == 0 else right_ref
        window[side, :, halo_at : halo_at + span] = halo_ref[:, :span]
        for row, p in enumerate((p0, p1, p2, p3)):
            window[side, row * COLS : (row + 1) * COLS, own_at : own_at + 2 * span] = p[
                :, base : base + 2 * span
            ]
    slot = 0
    for part in (0, 1):
        for pair in range(W // 2):
            results = []
            for e in (0, 1):
                local = 2 * pair + e
                t = local + part * (LEAVES - W)
                sources = []
                for k in range(NEAR):
                    start = pl.multiple_of((W + local + offset_ref[t, k]) * LEAF, LEAF)
                    sources.append(window[part, :, pl.ds(start, LEAF)])
                results.append(near_leaf(sources, blocks_ref, t))
            store_pair(out_refs, slot, results)
            slot += 1


NEAR_OUT = [jax.ShapeDtypeStruct((PAIRS // 2 * COLS, 6 * RANK), BF16)] * SIDES


def near_inner(offsets, pieces, blocks):
    return pl.pallas_call(
        inner_kernel,
        in_specs=[SMEM] + [VMEM] * 5,
        out_specs=[VMEM] * SIDES,
        out_shape=NEAR_OUT,
        compiler_params=params(16),
        cost_estimate=cost(2**28, 2**23),
        name="near_inner",
    )(offsets, *pieces, blocks)


def near_outer(offsets, pieces, left, right, blocks):
    return pl.pallas_call(
        outer_kernel,
        in_specs=[SMEM] + [VMEM] * 7,
        out_specs=[VMEM] * SIDES,
        out_shape=NEAR_OUT,
        scratch_shapes=[pltpu.VMEM((2, SIDES * COLS, 3 * W * LEAF), BF16)],
        compiler_params=params(16),
        cost_estimate=cost(2**28, 2**23),
        name="near_outer",
    )(offsets, *pieces, left, right, blocks)


def by_operator(flat):
    return jnp.concatenate([flat[:, o * RANK : (o + 1) * RANK] for o in range(OPS)], axis=0)


def half_of(children, odd):
    return jnp.where(odd == 1, children[:, RANK:], children[:, :RANK])


def far_kernel(
    where_ref,
    offset_ref,
    roots_ref,
    top_ref,
    root_coupling_ref,
    upper_ref,
    transfer_ref,
    pairs_ref,
    left_ref,
    right_ref,
    coupling_ref,
    basis_ref,
    out_ref,
    upper1,
    upper2,
    near_coef,
    sems,
):
    q = where_ref[0]
    copies = []
    for slot, (level, buffer) in enumerate(((1, upper1), (2, upper2))):
        row = (0, ROOTS // 2)[level - 1] + (q >> level)
        copy = pltpu.make_async_copy(upper_ref.at[:, row], buffer, sems.at[slot])
        copy.start()
        copies.append(copy)

    def spread(first, source):
        for i in range(source.shape[0] // COLS):
            both = source[i * COLS : (i + 1) * COLS, :]
            near_coef[first + 2 * i] = both[:, :RANK]
            near_coef[first + 2 * i + 1] = both[:, RANK:]

    spread(0, left_ref[:, W * LEAF :])
    spread(W, pairs_ref[...].reshape(PAIRS * COLS, 2 * RANK))
    spread(W + LEAVES, right_ref[:, W * LEAF :])

    def valid(c, height):
        return jnp.logical_and(c >= 0, c < (ROOTS >> height))

    def clip(c, height):
        return jnp.minimum(jnp.maximum(c, 0), (ROOTS >> height) - 1)

    def coef(height, c):
        if height == 0:
            return roots_ref[c]
        first = (0, ROOTS // 2)[height - 1]
        joined = jnp.concatenate([coef(height - 1, 2 * c), coef(height - 1, 2 * c + 1)], axis=1)
        return dot_nt(joined, top_ref[first + c]).astype(BF16)

    def sources(height):
        c = q >> height
        odd = c % 2
        parts = []
        for even_step, odd_step in ((-2, -3), (2, -2), (3, 2)):
            other = c + jnp.where(odd == 1, odd_step, even_step)
            value = coef(height, clip(other, height))
            parts.append(jnp.where(valid(other, height), value, jnp.zeros_like(value)))
        return jnp.concatenate(parts, axis=1)

    fields = [dot_nt(sources(0), root_coupling_ref[:, 0].reshape(OPS * RANK, 3 * RANK))]
    wide1, wide2 = sources(1), sources(2)
    copies[0].wait()
    copies[1].wait()
    fields.append(dot_nt(wide1, upper1[...].reshape(OPS * RANK, 3 * RANK)))
    fields.append(dot_nt(wide2, upper2[...].reshape(OPS * RANK, 3 * RANK)))

    running = by_operator(fields[2])
    children = dot_nn(running.astype(BF16), top_ref[ROOTS // 2 + (q >> 2)])
    running = by_operator(fields[1]) + half_of(children, (q >> 1) % 2)
    children = dot_nn(running.astype(BF16), top_ref[q >> 1])
    running = by_operator(fields[0]) + half_of(children, q % 2)

    level = [running]
    last = LEAVES - 1
    while len(level) < LEAVES:
        count = len(level)
        last -= count
        lower = []
        for i, value in enumerate(level):
            children = dot_nn(value.astype(BF16), transfer_ref[last + i])
            lower += [children[:, :RANK], children[:, RANK:]]
        level = lower

    for t in range(LEAVES):
        wide = jnp.concatenate([near_coef[W + t + offset_ref[t, k]] for k in range(FAR)], axis=1)
        coupled = dot_nt(wide, coupling_ref[:, t].reshape(OPS * RANK, FAR * RANK))
        field = (level[t] + by_operator(coupled)).astype(BF16)
        far = dot_nn(field, basis_ref[t])
        out_ref[:, :, t * LEAF : (t + 1) * LEAF] = far.reshape(OPS, COLS, LEAF)


def far_field(where, offsets, roots, top, root_coupling, upper, transfer, pairs, left, right, coupling, basis):
    return pl.pallas_call(
        far_kernel,
        in_specs=[SMEM, SMEM, VMEM, VMEM, VMEM, ANY] + [VMEM] * 6,
        out_specs=VMEM,
        out_shape=jax.ShapeDtypeStruct((OPS, COLS, LEAVES * LEAF), F32),
        scratch_shapes=[
            pltpu.VMEM((OPS, RANK, 3 * RANK), BF16),
            pltpu.VMEM((OPS, RANK, 3 * RANK), BF16),
            pltpu.VMEM((LEAVES + 2 * W, COLS, RANK), BF16),
            pltpu.SemaphoreType.DMA((2,)),
        ],
        compiler_params=params(16),
        cost_estimate=cost(2**27, 2**23),
        name="far_field",
    )(where, offsets, roots, top, root_coupling, upper, transfer, pairs, left, right, coupling, basis)


def join_kernel(where_ref, far_ref, *refs):
    inner, outer = refs[:SIDES], refs[SIDES : 2 * SIDES]
    out_ref, ordered = refs[2 * SIDES :]
    me = where_ref[0]
    half = PAIRS // 2 * COLS
    edge = W // 2 * COLS
    for step in range(SIDES):
        rows = lax.rem(me + SIDES - step, SIDES)
        ordered[rows, :edge] = outer[step][:edge]
        ordered[rows, edge : edge + half] = inner[step][...]
        ordered[rows, edge + half :] = outer[step][edge:]
    for pair in range(PAIRS):
        parts = [ordered[r, pair * COLS : (pair + 1) * COLS].astype(F32) for r in range(SIDES)]
        for e in (0, 1):
            for o in range(OPS):
                at = (e * OPS + o) * RANK
                near = jnp.concatenate([part[:, at : at + RANK] for part in parts], axis=1)
                columns = slice((2 * pair + e) * LEAF, (2 * pair + e + 1) * LEAF)
                out_ref[o, :, columns] = (far_ref[o, :, columns] + near).astype(BF16)


def join(where, far, inner, outer):
    return pl.pallas_call(
        join_kernel,
        in_specs=[SMEM] + [VMEM] * (1 + 2 * SIDES),
        out_specs=VMEM,
        out_shape=jax.ShapeDtypeStruct((OPS, COLS, LEAVES * LEAF), BF16),
        scratch_shapes=[pltpu.VMEM((SIDES, PAIRS * COLS, 6 * RANK), BF16)],
        compiler_params=params(8),
        cost_estimate=cost(2**20, 2**22),
        name="join",
    )(where, far, *inner, *outer)


def round_rhs(value, step):
    return lax.ppermute(value, "rhs", [(i, (i + step) % SIDES) for i in range(SIDES)])


def along_leaf(value, step):
    count = lax.axis_size("leaf")
    return lax.ppermute(
        value, "leaf", [(i, i + step) for i in range(count) if 0 <= i + step < count]
    )


def per_device(
    points,
    leaf_basis,
    local_transfer,
    top_transfer,
    leaf_coupling,
    root_coupling,
    upper_coupling,
    near_blocks,
    near_offset,
    far_offset,
):
    leaf_index = lax.axis_index("leaf").astype(jnp.int32).reshape(1)
    rhs_index = lax.axis_index("rhs").astype(jnp.int32).reshape(1)
    transfer = local_transfer[0]

    pieces = [points] + [round_rhs(points, -step) for step in range(1, SIDES)]
    pairs, root = upsweep(points, leaf_basis, transfer)
    roots = lax.all_to_all(root, "leaf", 0, 0, tiled=True).reshape(ROOTS, COLS, RANK)

    edge = W * LEAF
    tail = jnp.concatenate(
        [
            jnp.concatenate([p[:, -edge:] for p in pieces], axis=0),
            pairs[-W // 2 :].reshape(SIDES * COLS, 2 * RANK),
        ],
        axis=1,
    )
    head = jnp.concatenate(
        [
            jnp.concatenate([p[:, :edge] for p in pieces], axis=0),
            pairs[: W // 2].reshape(SIDES * COLS, 2 * RANK),
        ],
        axis=1,
    )
    left = along_leaf(tail, 1)
    right = along_leaf(head, -1)

    inner = near_inner(near_offset, pieces, near_blocks)
    inner = [inner[0]] + [round_rhs(inner[step], step) for step in range(1, SIDES)]
    outer = near_outer(near_offset, pieces, left, right, near_blocks)
    outer = [outer[0]] + [round_rhs(outer[step], step) for step in range(1, SIDES)]
    far = far_field(
        leaf_index,
        far_offset,
        roots,
        top_transfer,
        root_coupling,
        upper_coupling,
        transfer,
        pairs,
        left,
        right,
        leaf_coupling,
        leaf_basis,
    )
    return join(rhs_index, far, inner, outer)


def solution(mesh):
    placed = (
        P("rhs", "leaf"),
        P("leaf", None, None),
        P("leaf", None, None, None),
        P(),
        P(None, "leaf", None, None),
        P(None, "leaf", None, None),
        P(),
        P(None, "leaf", None, "rhs", None),
        P("leaf", None),
        P("leaf", None),
    )
    return jax.shard_map(
        per_device, mesh=mesh, in_specs=placed, out_specs=P(None, "rhs", "leaf"), check_vma=False
    )
```

time: 168 us -> 80.9 us (0.48)
  the two profiles are of different devices: /device:TPU:105 before, /device:TPU:8 now
where the time goes in v1:
time: 80.9 us; the launch traced here: 80.4 us
  starting transfers between devices  33 us (41%)
  Pallas kernels  23.6 us (29%)
  local copies, waits for them, and re-layouts  17.1 us (21%)
  waiting for transfers between devices  4.95 us (6%)
  other arithmetic  1.48 us (2%)
    unnamed x34, local copies, waits for them, and re-layouts  16.2 us
    ppermute x9, starting transfers between devices, round_rhs(): lax.ppermute(value, 'rhs', [(i, (i + step) % SIDES) for i in range(SIDES)])  14.5 us
    pallas_call x1, Pallas kernels, far_field(): pl.pallas_call(far_kernel, in_specs=[SMEM, SMEM, VMEM, VMEM, VMEM, ANY] +...  13.3 us
    all_to_all x1, starting transfers between devices, per_device(): lax.all_to_all(root, 'leaf', 0, 0, tiled=True).reshape(ROOTS, COLS, RANK)  13 us
    ppermute x2, starting transfers between devices, along_leaf(): lax.ppermute(value, 'leaf', [(i, i + step) for i in range(count) if 0 <=...  5.54 us
    ppermute x9, waiting for transfers between devices, round_rhs(): lax.ppermute(value, 'rhs', [(i, (i + step) % SIDES) for i in range(SIDES)])  4.94 us
    pallas_call x1, Pallas kernels, near_outer(): pl.pallas_call(outer_kernel, in_specs=[SMEM] + [VMEM] * 7, out_specs=[VME...  3.26 us
    pallas_call x1, Pallas kernels, near_inner(): pl.pallas_call(inner_kernel, in_specs=[SMEM] + [VMEM] * 5, out_specs=[VME...  3.17 us
  transfers between devices with their start and end apart: 12, of which 1 were waited for; matrix products, arithmetic and copies ran while one was open for 6% of the time, Pallas kernels for 26%

profile of v1, /device:TPU:8, one launch (start us, length us, event | category | flops | bytes accessed | tf_op | source)
XLA Modules:
  0.0 80.4 jit_solution(6825851682926633941)
XLA Ops:
  0.0 0.0 copy-start.7
  0.0 1.5 %collective-permute-start.2 = (bf16[16,8192]{1,0:T(8,128)(2,1)}, bf16[16,8192]{1,0:T(8,128)(2,1)S(1)}, u32[]{:S(2)}, u32[]{:S(2)}) collective-permute-start(bf16[16,8192]{1,0:T(8,128)(2,1)} %p0.3), channel_id=1, source_target_pairs={{0,1},{1,2},{2,3},{3,0},{4,5},{5,6},{6,7},{7,4},{8,9},{9,10},{10,1... | collective-permute-start | bytes 786440 | tf_op jit(solution)/shard_map/ppermute | solution.py:325
  1.5 2.7 %collective-permute-start.1 = (bf16[16,8192]{1,0:T(8,128)(2,1)}, bf16[16,8192]{1,0:T(8,128)(2,1)S(1)}, u32[]{:S(2)}, u32[]{:S(2)}) collective-permute-start(bf16[16,8192]{1,0:T(8,128)(2,1)} %p0.3), channel_id=1, source_target_pairs={{0,2},{1,3},{2,0},{3,1},{4,6},{5,7},{6,4},{7,5},{8,10},{9,11},{10,... | collective-permute-start | bytes 786440 | tf_op jit(solution)/shard_map/ppermute | solution.py:325
  4.2 1.4 %collective-permute-start = (bf16[16,8192]{1,0:T(8,128)(2,1)}, bf16[16,8192]{1,0:T(8,128)(2,1)S(1)}, u32[]{:S(2)}, u32[]{:S(2)}) collective-permute-start(bf16[16,8192]{1,0:T(8,128)(2,1)} %p0.3), channel_id=1, source_target_pairs={{0,3},{1,0},{2,1},{3,2},{4,7},{5,4},{6,5},{7,6},{8,11},{9,8},{10,9... | collective-permute-start | bytes 786440 | tf_op jit(solution)/shard_map/ppermute | solution.py:325
  5.7 0.9 %fusion = (bf16[16,2048]{1,0:T(8,128)(2,1)S(1)}, bf16[16,2048]{1,0:T(8,128)(2,1)S(1)}) fusion(bf16[16,8192]{1,0:T(8,128)(2,1)} %p0.3), kind=kLoop, calls=%fused_computation.2 | loop fusion | bytes 262144 | tf_op jit(solution)/shard_map/slice | solution.py:365
  6.5 0.0 copy-start.4
  6.6 1.2 %copy-done.4 = bf16[32,64,256]{2,1,0:T(8,128)(2,1)S(1)} copy-done((bf16[32,64,256]{2,1,0:T(8,128)(2,1)S(1)}, bf16[32,64,256]{2,1,0:T(8,128)(2,1)}, u32[]{:S(2)}) %copy-start.4) | copy-done | bytes 1048600
  7.8 0.0 copy-start.6
  7.8 0.9 %copy-done.6 = bf16[16,8192]{1,0:T(8,128)(2,1)S(1)} copy-done((bf16[16,8192]{1,0:T(8,128)(2,1)S(1)}, bf16[16,8192]{1,0:T(8,128)(2,1)}, u32[]{:S(2)}) %copy-start.6) | copy-done | bytes 262168
  8.7 0.0 copy-start.8
  8.7 1.0 %copy-done.8 = bf16[1,31,64,128]{3,2,1,0:T(8,128)(2,1)S(1)} copy-done((bf16[1,31,64,128]{3,2,1,0:T(8,128)(2,1)S(1)}, bf16[1,31,64,128]{3,2,1,0:T(8,128)(2,1)}, u32[]{:S(2)}) %copy-start.8) | copy-done | bytes 507928
  9.8 1.3 %upsweep.1 = (bf16[16,16,128]{2,1,0:T(8,128)(2,1)S(1)}, bf16[1024,64]{1,0:T(8,128)(2,1)S(1)}) custom-call(bf16[16,8192]{1,0:T(8,128)(2,1)S(1)} %copy-done.6, bf16[32,64,256]{2,1,0:T(8,128)(2,1)S(1)} %copy-done.4, bf16[31,64,128]{2,1,0:T(8,128)(2,1)S(1)} %bitcast.6), custom_call_target="tpu_custom_call" | custom-call | flops 33554432 | bytes 2097152 | tf_op jit(solution)/shard_map/upsweep/pallas_call | solution.py:74
  11.1 0.0 collective-permute-done.2.p3
  11.2 4.9 %collective-permute-done.1.p2 = bf16[16,8192]{1,0:T(8,128)(2,1)S(1)} collective-permute-done((bf16[16,8192]{1,0:T(8,128)(2,1)}, bf16[16,8192]{1,0:T(8,128)(2,1)S(1)}, u32[]{:S(2)}, u32[]{:S(2)}) %collective-permute-start.1) | collective-permute-done | bytes 262176 | tf_op jit(solution)/shard_map/ppermute | solution.py:325
  16.1 0.0 collective-permute-done.p1
  16.1 0.7 pad_maximum_fusion
  16.8 1.9 %collective-permute-start.3 = (bf16[64,2176]{1,0:T(8,128)(2,1)}, bf16[64,2176]{1,0:T(8,128)(2,1)S(1)}, u32[]{:S(2)}, u32[]{:S(2)}) collective-permute-start(bf16[64,2176]{1,0:T(8,128)(2,1)} %pad_maximum_fusion), channel_id=1, source_target_pairs={{0,4},{4,8},{8,12},{12,16},{16,20},{20,24},{24,28},{28,32},{32,36}... | collective-permute-start | bytes 835592 | tf_op jit(solution)/shard_map/ppermute | solution.py:330
  18.8 0.7 pad_maximum_fusion.1
  19.5 3.6 %collective-permute-start.4 = (bf16[64,2176]{1,0:T(8,128)(2,1)}, bf16[64,2176]{1,0:T(8,128)(2,1)S(1)}, u32[]{:S(2)}, u32[]{:S(2)}) collective-permute-start(bf16[64,2176]{1,0:T(8,128)(2,1)} %pad_maximum_fusion.1), channel_id=1, source_target_pairs={{4,0},{8,4},{12,8},{16,12},{20,16},{24,20},{28,24},{32,28},{36,32}... | collective-permute-start | bytes 835592 | tf_op jit(solution)/shard_map/ppermute | solution.py:330
  23.1 0.8 %reshape.20 = bf16[64,2,512]{2,1,0:T(2,128)(2,1)} reshape(bf16[64,16,64]{2,1,0:T(8,128)(2,1)S(1)} %bitcast.8) | data formatting | bytes 262144
  24.0 13.0 %all-to-all-start = ((bf16[64,2,512]{2,1,0:T(2,128)(2,1)}), bf16[64,2,512]{2,1,0:T(2,128)(2,1)}, u32[]{:S(2)}, u32[]{:S(2)}) async-start(bf16[64,2,512]{2,1,0:T(2,128)(2,1)} %reshape.20), calls=%async_computation | async-start | bytes 262144 | tf_op jit(solution)/shard_map/all_to_all | solution.py:353
  37.0 0.8 copy.12.offset_ref
  37.7 0.0 copy-done.7
  37.7 0.0 copy-start
  37.7 3.7 %copy-done = bf16[3,32,3,64,256]{4,3,2,1,0:T(8,128)(2,1)S(1)} copy-done((bf16[3,32,3,64,256]{4,3,2,1,0:T(8,128)(2,1)S(1)}, bf16[3,32,3,64,256]{4,3,2,1,0:T(8,128)(2,1)}, u32[]{:S(2)}) %copy-start) | copy-done | bytes 9437208
  41.4 0.0 copy-start.1
  41.4 3.2 %near_inner.1 = (bf16[128,384]{1,0:T(8,128)(2,1)S(1)}, bf16[128,384]{1,0:T(8,128)(2,1)S(1)}, bf16[128,384]{1,0:T(8,128)(2,1)}, bf16[128,384]{1,0:T(8,128)(2,1)}) custom-call(s32[32,3]{1,0:T(8,128)S(1)} %copy.12.offset_ref, bf16[16,8192]{1,0:T(8,128)(2,1)S(1)} %copy-done.7, bf16[16,8192]{1,0:T(8,128)(2,1)S(1)} %collective-permute-done.p1, ...), custom_call_target="tpu_custom_call" | custom-call | flops 268435456 | bytes 8388608 | tf_op jit(solution)/shard_map/near_inner/pallas_call | solution.py:148
  44.6 1.3 %collective-permute-start.5 = (bf16[128,384]{1,0:T(8,128)(2,1)S(1)}, bf16[128,384]{1,0:T(8,128)(2,1)S(1)}, u32[]{:S(2)}, u32[]{:S(2)}) collective-permute-start(bf16[128,384]{1,0:T(8,128)(2,1)S(1)} %get-tuple-element.18), channel_id=1, source_target_pairs={{0,1},{1,2},{2,3},{3,0},{4,5},{5,6},{6,7},{7,4},{8,9},{9,10},{10,1... | collective-permute-start | bytes 294920 | tf_op jit(solution)/shard_map/ppermute | solution.py:325
  45.9 2.4 %collective-permute-start.6 = (bf16[128,384]{1,0:T(8,128)(2,1)}, bf16[128,384]{1,0:T(8,128)(2,1)}, u32[]{:S(2)}, u32[]{:S(2)}) collective-permute-start(bf16[128,384]{1,0:T(8,128)(2,1)} %get-tuple-element.19), channel_id=1, source_target_pairs={{0,2},{1,3},{2,0},{3,1},{4,6},{5,7},{6,4},{7,5},{8,10},{9,11},{10,... | collective-permute-start | bytes 294920 | tf_op jit(solution)/shard_map/ppermute | solution.py:325
  48.3 0.0 copy-start.14
  48.3 0.0 copy-start.5
  48.3 0.0 copy-start.9
  48.3 0.0 copy-start.11
  48.3 1.6 %collective-permute-start.7 = (bf16[128,384]{1,0:T(8,128)(2,1)}, bf16[128,384]{1,0:T(8,128)(2,1)}, u32[]{:S(2)}, u32[]{:S(2)}) collective-permute-start(bf16[128,384]{1,0:T(8,128)(2,1)} %get-tuple-element.20), channel_id=1, source_target_pairs={{0,3},{1,0},{2,1},{3,2},{4,7},{5,4},{6,5},{7,6},{8,11},{9,8},{10,9... | collective-permute-start | bytes 294920 | tf_op jit(solution)/shard_map/ppermute | solution.py:325
  49.9 0.0 collective-permute-done.3.left_ref
  49.9 0.0 collective-permute-done.4.right_ref
  49.9 0.0 copy-done.1
  50.0 3.3 %near_outer.1 = (bf16[128,384]{1,0:T(8,128)(2,1)S(1)}, bf16[128,384]{1,0:T(8,128)(2,1)}, bf16[128,384]{1,0:T(8,128)(2,1)}, bf16[128,384]{1,0:T(8,128)(2,1)}) custom-call(s32[32,3]{1,0:T(8,128)S(1)} %copy.12.offset_ref, bf16[16,8192]{1,0:T(8,128)(2,1)S(1)} %copy-done.7, bf16[16,8192]{1,0:T(8,128)(2,1)S(1)} %collective-permute-done.p1, ...), custom_call_target="tpu_custom_call" | custom-call | flops 268435456 | bytes 8388608 | tf_op jit(solution)/shard_map/near_outer/pallas_call | solution.py:160
  53.2 0.0 copy-start.12
  53.2 0.6 copy-done.12
  53.9 0.5 collective-permute-start.8
  54.3 1.1 %collective-permute-start.9 = (bf16[128,384]{1,0:T(8,128)(2,1)}, bf16[128,384]{1,0:T(8,128)(2,1)}, u32[]{:S(2)}, u32[]{:S(2)}) collective-permute-start(bf16[128,384]{1,0:T(8,128)(2,1)} %get-tuple-element.23), channel_id=1, source_target_pairs={{0,2},{1,3},{2,0},{3,1},{4,6},{5,7},{6,4},{7,5},{8,10},{9,11},{10,... | collective-permute-start | bytes 294920 | tf_op jit(solution)/shard_map/ppermute | solution.py:325
  55.5 0.0 collective-permute-done.5.refs_1_
  55.5 1.9 %collective-permute-start.10 = (bf16[128,384]{1,0:T(8,128)(2,1)}, bf16[128,384]{1,0:T(8,128)(2,1)}, u32[]{:S(2)}, u32[]{:S(2)}) collective-permute-start(bf16[128,384]{1,0:T(8,128)(2,1)} %get-tuple-element.24), channel_id=1, source_target_pairs={{0,3},{1,0},{2,1},{3,2},{4,7},{5,4},{6,5},{7,6},{8,11},{9,8},{10,9... | collective-permute-start | bytes 294920 | tf_op jit(solution)/shard_map/ppermute | solution.py:325
  57.4 0.0 copy-done.14
  57.4 0.1 copy.11.offset_ref
  57.5 0.0 all-to-all-done
  57.5 1.1 %reshape.21.roots_ref = bf16[64,16,64]{2,1,0:T(8,128)(2,1)S(1)} reshape(bf16[64,2,512]{2,1,0:T(2,128)(2,1)} %all-to-all-done) | data formatting | bytes 262144
  58.6 0.0 copy-done.5
  58.6 0.0 copy-done.9
  58.7 0.0 copy-done.11
  58.7 0.0 copy-start.2
  58.7 2.3 %copy-done.2 = bf16[3,48,64,192]{3,2,1,0:T(8,128)(2,1)S(1)} copy-done((bf16[3,48,64,192]{3,2,1,0:T(8,128)(2,1)S(1)}, bf16[3,48,64,192]{3,2,1,0:T(8,128)(2,1)}, u32[]{:S(2)}) %copy-start.2) | copy-done | bytes 3538968
  61.0 0.0 copy-start.3
  61.0 2.3 %copy-done.3 = bf16[3,32,64,320]{3,2,1,0:T(8,128)(2,1)S(1)} copy-done((bf16[3,32,64,320]{3,2,1,0:T(8,128)(2,1)S(1)}, bf16[3,32,64,320]{3,2,1,0:T(8,128)(2,1)}, u32[]{:S(2)}) %copy-start.3) | copy-done | bytes 3932184
  63.3 1.1 %copy-done.10 = bf16[48,64,128]{2,1,0:T(8,128)(2,1)S(1)} copy-done((bf16[48,64,128]{2,1,0:T(8,128)(2,1)S(1)}, bf16[48,64,128]{2,1,0:T(8,128)(2,1)}, u32[]{:S(2)}) %copy-start.10) | copy-done | bytes 786456
  64.5 13.3 %far_field.1.far_ref = f32[3,16,8192]{2,1,0:T(8,128)S(1)} custom-call(s32[1]{0:T(128)} %bitcast.1.where_ref, s32[32,5]{1,0:T(8,128)S(1)} %copy.11.offset_ref, bf16[64,16,64]{2,1,0:T(8,128)(2,1)S(1)} %reshape.21.roots_ref, bf16[48,64,128]{2,1,0:T(8,128)(2,1)S(1)} %copy-done.10, bf16[3,1,64,192]{3,2,1,0:T(8,128)(2,1)S(1)} %copy-done.11, ...), custom_call_target="tpu_custom_call" | custom-call | flops 134217728 | bytes 8388608 | tf_op jit(solution)/shard_map/far_field/pallas_call | solution.py:273
  77.8 0.0 collective-permute-done.6.refs_2_
  77.8 0.0 collective-permute-done.7.refs_3_
  77.8 0.0 collective-permute-done.8.refs_5_
  77.8 0.0 collective-permute-done.9.refs_6_
  77.9 0.0 collective-permute-done.10.refs_7_
  77.9 0.0 copy-done.13
  77.9 2.5 %join.1 = bf16[3,16,8192]{2,1,0:T(8,128)(2,1)} custom-call(s32[1]{0:T(128)} %bitcast.where_ref, f32[3,16,8192]{2,1,0:T(8,128)S(1)} %far_field.1.far_ref, bf16[128,384]{1,0:T(8,128)(2,1)S(1)} %get-tuple-element.17.refs_0_, bf16[128,384]{1,0:T(8,128)(2,1)S(1)} %collective-permute-done.5.refs_1_, bf16[128,384]{1,0:T(8,128)(2,1)} %collective-permute-done.6.refs_2_, ...), custom_call_target="tpu_custom_call" | custom-call | flops 1048576 | bytes 4194304 | tf_op jit(solution)/shard_map/join/pallas_call | solution.py:312
  (6 shorter events, 0.0 us)
Async XLA Ops:
  0.0 37.7 %copy-start.7 = (bf16[16,8192]{1,0:T(8,128)(2,1)S(1)}, bf16[16,8192]{1,0:T(8,128)(2,1)}, u32[]{:S(2)}) copy-start(bf16[16,8192]{1,0:T(8,128)(2,1)} %p0.3) | copy-start | bytes 786436
  0.0 11.1 %collective-permute-start.2 = (bf16[16,8192]{1,0:T(8,128)(2,1)}, bf16[16,8192]{1,0:T(8,128)(2,1)S(1)}, u32[]{:S(2)}, u32[]{:S(2)}) collective-permute-start(bf16[16,8192]{1,0:T(8,128)(2,1)} %p0.3), channel_id=1, source_target_pairs={{0,1},{1,2},{2,3},{3,0},{4,5},{5,6},{6,7},{7,4},{8,9},{9,10},{10,1... | collective-permute-start | bytes 786440 | tf_op jit(solution)/shard_map/ppermute | solution.py:325
  1.5 14.6 %collective-permute-start.1 = (bf16[16,8192]{1,0:T(8,128)(2,1)}, bf16[16,8192]{1,0:T(8,128)(2,1)S(1)}, u32[]{:S(2)}, u32[]{:S(2)}) collective-permute-start(bf16[16,8192]{1,0:T(8,128)(2,1)} %p0.3), channel_id=1, source_target_pairs={{0,2},{1,3},{2,0},{3,1},{4,6},{5,7},{6,4},{7,5},{8,10},{9,11},{10,... | collective-permute-start | bytes 786440 | tf_op jit(solution)/shard_map/ppermute | solution.py:325
  4.2 11.9 %collective-permute-start = (bf16[16,8192]{1,0:T(8,128)(2,1)}, bf16[16,8192]{1,0:T(8,128)(2,1)S(1)}, u32[]{:S(2)}, u32[]{:S(2)}) collective-permute-start(bf16[16,8192]{1,0:T(8,128)(2,1)} %p0.3), channel_id=1, source_target_pairs={{0,3},{1,0},{2,1},{3,2},{4,7},{5,4},{6,5},{7,6},{8,11},{9,8},{10,9... | collective-permute-start | bytes 786440 | tf_op jit(solution)/shard_map/ppermute | solution.py:325
  6.5 1.2 %copy-start.4 = (bf16[32,64,256]{2,1,0:T(8,128)(2,1)S(1)}, bf16[32,64,256]{2,1,0:T(8,128)(2,1)}, u32[]{:S(2)}) copy-start(bf16[32,64,256]{2,1,0:T(8,128)(2,1)} %basis_ref.3) | copy-start | bytes 3145732
  7.8 0.9 %copy-start.6 = (bf16[16,8192]{1,0:T(8,128)(2,1)S(1)}, bf16[16,8192]{1,0:T(8,128)(2,1)}, u32[]{:S(2)}) copy-start(bf16[16,8192]{1,0:T(8,128)(2,1)} %p0.3) | copy-start | bytes 786436
  8.7 1.0 %copy-start.8 = (bf16[1,31,64,128]{3,2,1,0:T(8,128)(2,1)S(1)}, bf16[1,31,64,128]{3,2,1,0:T(8,128)(2,1)}, u32[]{:S(2)}) copy-start(bf16[1,31,64,128]{3,2,1,0:T(8,128)(2,1)} %param.12) | copy-start | bytes 1523716
  16.8 33.1 %collective-permute-start.3 = (bf16[64,2176]{1,0:T(8,128)(2,1)}, bf16[64,2176]{1,0:T(8,128)(2,1)S(1)}, u32[]{:S(2)}, u32[]{:S(2)}) collective-permute-start(bf16[64,2176]{1,0:T(8,128)(2,1)} %pad_maximum_fusion), channel_id=1, source_target_pairs={{0,4},{4,8},{8,12},{12,16},{16,20},{20,24},{24,28},{28,32},{32,36}... | collective-permute-start | bytes 835592 | tf_op jit(solution)/shard_map/ppermute | solution.py:330
  19.5 30.4 %collective-permute-start.4 = (bf16[64,2176]{1,0:T(8,128)(2,1)}, bf16[64,2176]{1,0:T(8,128)(2,1)S(1)}, u32[]{:S(2)}, u32[]{:S(2)}) collective-permute-start(bf16[64,2176]{1,0:T(8,128)(2,1)} %pad_maximum_fusion.1), channel_id=1, source_target_pairs={{4,0},{8,4},{12,8},{16,12},{20,16},{24,20},{28,24},{32,28},{36,32}... | collective-permute-start | bytes 835592 | tf_op jit(solution)/shard_map/ppermute | solution.py:330
  24.0 33.5 %all-to-all-start = ((bf16[64,2,512]{2,1,0:T(2,128)(2,1)}), bf16[64,2,512]{2,1,0:T(2,128)(2,1)}, u32[]{:S(2)}, u32[]{:S(2)}) async-start(bf16[64,2,512]{2,1,0:T(2,128)(2,1)} %reshape.20), calls=%async_computation | async-start | bytes 262144 | tf_op jit(solution)/shard_map/all_to_all | solution.py:353
  37.7 3.7 %copy-start = (bf16[3,32,3,64,256]{4,3,2,1,0:T(8,128)(2,1)S(1)}, bf16[3,32,3,64,256]{4,3,2,1,0:T(8,128)(2,1)}, u32[]{:S(2)}) copy-start(bf16[3,32,3,64,256]{4,3,2,1,0:T(8,128)(2,1)} %blocks_ref.3) | copy-start | bytes 28311556
  41.4 8.5 %copy-start.1 = (bf16[3,32,3,64,256]{4,3,2,1,0:T(8,128)(2,1)S(1)}, bf16[3,32,3,64,256]{4,3,2,1,0:T(8,128)(2,1)}, u32[]{:S(2)}) copy-start(bf16[3,32,3,64,256]{4,3,2,1,0:T(8,128)(2,1)} %blocks_ref.3) | copy-start | bytes 28311556
  44.6 10.9 %collective-permute-start.5 = (bf16[128,384]{1,0:T(8,128)(2,1)S(1)}, bf16[128,384]{1,0:T(8,128)(2,1)S(1)}, u32[]{:S(2)}, u32[]{:S(2)}) collective-permute-start(bf16[128,384]{1,0:T(8,128)(2,1)S(1)} %get-tuple-element.18), channel_id=1, source_target_pairs={{0,1},{1,2},{2,3},{3,0},{4,5},{5,6},{6,7},{7,4},{8,9},{9,10},{10,1... | collective-permute-start | bytes 294920 | tf_op jit(solution)/shard_map/ppermute | solution.py:325
  45.9 31.9 %collective-permute-start.6 = (bf16[128,384]{1,0:T(8,128)(2,1)}, bf16[128,384]{1,0:T(8,128)(2,1)}, u32[]{:S(2)}, u32[]{:S(2)}) collective-permute-start(bf16[128,384]{1,0:T(8,128)(2,1)} %get-tuple-element.19), channel_id=1, source_target_pairs={{0,2},{1,3},{2,0},{3,1},{4,6},{5,7},{6,4},{7,5},{8,10},{9,11},{10,... | collective-permute-start | bytes 294920 | tf_op jit(solution)/shard_map/ppermute | solution.py:325
  48.3 9.1 %copy-start.14 = (s32[32,5]{0,1:T(8,128)S(1)}, s32[32,5]{0,1:T(8,128)}, u32[]{:S(2)}) copy-start(s32[32,5]{0,1:T(8,128)} %param.19) | copy-start | bytes 1924
  48.3 10.4 %copy-start.5 = (bf16[32,64,256]{2,1,0:T(8,128)(2,1)S(1)}, bf16[32,64,256]{2,1,0:T(8,128)(2,1)}, u32[]{:S(2)}) copy-start(bf16[32,64,256]{2,1,0:T(8,128)(2,1)} %basis_ref.3) | copy-start | bytes 3145732
  48.3 10.4 %copy-start.9 = (bf16[1,31,64,128]{3,2,1,0:T(8,128)(2,1)S(1)}, bf16[1,31,64,128]{3,2,1,0:T(8,128)(2,1)}, u32[]{:S(2)}) copy-start(bf16[1,31,64,128]{3,2,1,0:T(8,128)(2,1)} %param.12) | copy-start | bytes 1523716
  48.3 10.4 %copy-start.11 = (bf16[3,1,64,192]{3,2,1,0:T(8,128)(2,1)S(1)}, bf16[3,1,64,192]{3,2,1,0:T(8,128)(2,1)}, u32[]{:S(2)}) copy-start(bf16[3,1,64,192]{3,2,1,0:T(8,128)(2,1)} %root_coupling_ref.1) | copy-start | bytes 221188
  48.3 29.5 %collective-permute-start.7 = (bf16[128,384]{1,0:T(8,128)(2,1)}, bf16[128,384]{1,0:T(8,128)(2,1)}, u32[]{:S(2)}, u32[]{:S(2)}) collective-permute-start(bf16[128,384]{1,0:T(8,128)(2,1)} %get-tuple-element.20), channel_id=1, source_target_pairs={{0,3},{1,0},{2,1},{3,2},{4,7},{5,4},{6,5},{7,6},{8,11},{9,8},{10,9... | collective-permute-start | bytes 294920 | tf_op jit(solution)/shard_map/ppermute | solution.py:325
  53.2 0.7 copy-start.12
  53.9 24.0 %collective-permute-start.8 = (bf16[128,384]{1,0:T(8,128)(2,1)}, bf16[128,384]{1,0:T(8,128)(2,1)}, u32[]{:S(2)}, u32[]{:S(2)}) collective-permute-start(bf16[128,384]{1,0:T(8,128)(2,1)} %get-tuple-element.22), channel_id=1, source_target_pairs={{0,1},{1,2},{2,3},{3,0},{4,5},{5,6},{6,7},{7,4},{8,9},{9,10},{10,1... | collective-permute-start | bytes 294920 | tf_op jit(solution)/shard_map/ppermute | solution.py:325
  54.3 23.5 %collective-permute-start.9 = (bf16[128,384]{1,0:T(8,128)(2,1)}, bf16[128,384]{1,0:T(8,128)(2,1)}, u32[]{:S(2)}, u32[]{:S(2)}) collective-permute-start(bf16[128,384]{1,0:T(8,128)(2,1)} %get-tuple-element.23), channel_id=1, source_target_pairs={{0,2},{1,3},{2,0},{3,1},{4,6},{5,7},{6,4},{7,5},{8,10},{9,11},{10,... | collective-permute-start | bytes 294920 | tf_op jit(solution)/shard_map/ppermute | solution.py:325
  55.5 22.4 %collective-permute-start.10 = (bf16[128,384]{1,0:T(8,128)(2,1)}, bf16[128,384]{1,0:T(8,128)(2,1)}, u32[]{:S(2)}, u32[]{:S(2)}) collective-permute-start(bf16[128,384]{1,0:T(8,128)(2,1)} %get-tuple-element.24), channel_id=1, source_target_pairs={{0,3},{1,0},{2,1},{3,2},{4,7},{5,4},{6,5},{7,6},{8,11},{9,8},{10,9... | collective-permute-start | bytes 294920 | tf_op jit(solution)/shard_map/ppermute | solution.py:325
  58.7 2.3 %copy-start.2 = (bf16[3,48,64,192]{3,2,1,0:T(8,128)(2,1)S(1)}, bf16[3,48,64,192]{3,2,1,0:T(8,128)(2,1)}, u32[]{:S(2)}) copy-start(bf16[3,48,64,192]{3,2,1,0:T(8,128)(2,1)} %upper_ref.1) | copy-start | bytes 10616836
  61.0 2.3 %copy-start.3 = (bf16[3,32,64,320]{3,2,1,0:T(8,128)(2,1)S(1)}, bf16[3,32,64,320]{3,2,1,0:T(8,128)(2,1)}, u32[]{:S(2)}) copy-start(bf16[3,32,64,320]{3,2,1,0:T(8,128)(2,1)} %coupling_ref.1) | copy-start | bytes 11796484
  63.3 1.1 %copy-start.10 = (bf16[48,64,128]{2,1,0:T(8,128)(2,1)S(1)}, bf16[48,64,128]{2,1,0:T(8,128)(2,1)}, u32[]{:S(2)}) copy-start(bf16[48,64,128]{2,1,0:T(8,128)(2,1)} %top_ref.1) | copy-start | bytes 2359300
  64.5 13.4 %copy-start.13 = (bf16[128,384]{1,0:T(8,128)(2,1)S(1)}, bf16[128,384]{1,0:T(8,128)(2,1)}, u32[]{:S(2)}) copy-start(bf16[128,384]{1,0:T(8,128)(2,1)} %copy-done.12) | copy-start | bytes 294916

commit v2 on v1

v2 whole, which is shorter than its diff:
```python
import functools

import jax
import jax.numpy as jnp
from jax import lax
from jax.experimental import pallas as pl
from jax.experimental.pallas import tpu as pltpu
from jax.sharding import PartitionSpec as P

LEAF = 256
RANK = 64
OPS = 3
W = 8
NEAR = 3
FAR = 5
TOPL = 3
COLS = 16
LEAVES = 32
ROOTS = 64
WINDOW = 32
SIDES = 4
PAIRS = LEAVES // 2
HALO = W * LEAF + 2 * RANK

NT = (((1,), (1,)), ((), ()))
NN = (((1,), (0,)), ((), ()))
F32 = jnp.float32
BF16 = jnp.bfloat16

VMEM = pl.BlockSpec(memory_space=pltpu.VMEM)
SMEM = pl.BlockSpec(memory_space=pltpu.SMEM)
ANY = pl.BlockSpec(memory_space=pl.ANY)
HBM = pl.BlockSpec(memory_space=pltpu.HBM)


def dot_nt(a, b):
    return lax.dot_general(a, b, NT, preferred_element_type=F32)


def dot_nn(a, b):
    return lax.dot_general(a, b, NN, preferred_element_type=F32)


def params(mib):
    return pltpu.CompilerParams(vmem_limit_bytes=mib * 2**20)


def in_hbm(value):
    return pltpu.with_memory_space_constraint(value, pltpu.HBM)


def cost(flops, bytes_accessed):
    return pl.CostEstimate(flops=flops, bytes_accessed=bytes_accessed, transcendentals=0)


def like(shape, dtype=BF16):
    return jax.ShapeDtypeStruct(shape, dtype)


class Staged:
    def __init__(self, moves, sems, ahead):
        self.copies = [pltpu.make_async_copy(a, b, sems.at[i]) for i, (a, b) in enumerate(moves)]
        self.started = 0
        self.waited = 0
        self.ahead = ahead
        self.fill()

    def fill(self):
        while self.started < min(len(self.copies), self.waited + self.ahead):
            self.copies[self.started].start()
            self.started += 1

    def wait(self, upto):
        while self.waited <= upto:
            self.copies[self.waited].wait()
            self.waited += 1
            self.fill()


UP_CUT = 16


def up_kernel(points_hbm, basis_hbm, transfer_hbm, pairs_ref, root_ref, points, basis, transfer, sems):
    moves = [(points_hbm, points)]
    for first in range(0, LEAVES, UP_CUT):
        rows = pl.ds(first, UP_CUT)
        moves.append((basis_hbm.at[rows], basis.at[rows]))
    moves.append((transfer_hbm, transfer))
    staged = Staged(moves, sems, 8)
    level = []
    for pair in range(PAIRS):
        staged.wait(1 + 2 * pair // UP_CUT)
        halves = [
            dot_nt(points[:, t * LEAF : (t + 1) * LEAF], basis[t])
            for t in (2 * pair, 2 * pair + 1)
        ]
        joined = jnp.concatenate(halves, axis=1).astype(BF16)
        pairs_ref[pair * COLS : (pair + 1) * COLS] = joined
        level.append(joined)
    staged.wait(len(moves) - 1)
    first = 0
    while True:
        parents = [dot_nt(joined, transfer[first + i]) for i, joined in enumerate(level)]
        first += len(level)
        if len(parents) == 1:
            break
        level = [
            jnp.concatenate(parents[i : i + 2], axis=1).astype(BF16)
            for i in range(0, len(parents), 2)
        ]
    root_ref[0] = parents[0].astype(BF16)


def upsweep(points, leaf_basis, transfer):
    return pl.pallas_call(
        up_kernel,
        in_specs=[HBM] * 3,
        out_specs=[VMEM] * 2,
        out_shape=[like((PAIRS * COLS, 2 * RANK)), like((1, COLS, RANK))],
        scratch_shapes=[
            pltpu.VMEM(points.shape, BF16),
            pltpu.VMEM(leaf_basis.shape, BF16),
            pltpu.VMEM(transfer.shape, BF16),
            pltpu.SemaphoreType.DMA((2 + LEAVES // UP_CUT,)),
        ],
        compiler_params=params(8),
        cost_estimate=cost(2**33, 2**20),
        name="upsweep",
    )(in_hbm(points), in_hbm(leaf_basis), in_hbm(transfer))


def pack_kernel(p0, p1, p2, p3, pairs_ref, after_ref, head_ref, tail_ref):
    del after_ref
    span = W * LEAF
    for row, p in enumerate((p0, p1, p2, p3)):
        rows = slice(row * COLS, (row + 1) * COLS)
        head_ref[rows, :span] = p[:, :span]
        tail_ref[rows, :span] = p[:, LEAVES * LEAF - span :]
    edge = W // 2 * COLS
    head_ref[:, span:] = pairs_ref[:edge]
    tail_ref[:, span:] = pairs_ref[PAIRS * COLS - edge :]


def pack_halos(pieces, pairs, after):
    return pl.pallas_call(
        pack_kernel,
        in_specs=[VMEM] * (SIDES + 1) + [ANY],
        out_specs=[VMEM] * 2,
        out_shape=[like((SIDES * COLS, HALO))] * 2,
        compiler_params=params(4),
        cost_estimate=cost(2**33, 2**20),
        name="pack_halos",
    )(*pieces, pairs, after)


def append_kernel(first_ref, second_ref, after_ref, out_ref):
    del after_ref
    count = first_ref.shape[0]
    out_ref[:count] = first_ref[...]
    out_ref[count:] = second_ref[...]


def append(first, second, after):
    return pl.pallas_call(
        append_kernel,
        in_specs=[VMEM] * 2 + [ANY],
        out_specs=VMEM,
        out_shape=like((2 * first.shape[0], COLS, RANK)),
        compiler_params=params(4),
        cost_estimate=cost(0, 0),
        name="append",
    )(first, second, after)


def near_leaf(sources, blocks_ref, t):
    wide = jnp.concatenate(sources, axis=1)
    block = jnp.concatenate(
        [blocks_ref[:, t, k].reshape(OPS * RANK, LEAF) for k in range(NEAR)], axis=1
    )
    return dot_nt(wide, block)


def store_pair(out_refs, slot, results):
    both = jnp.concatenate(results, axis=1).astype(BF16)
    for side, out_ref in enumerate(out_refs):
        out_ref[slot * COLS : (slot + 1) * COLS] = both[side * COLS : (side + 1) * COLS]


def near_kernel(offset_ref, p0, p1, p2, p3, left_ref, right_ref, blocks_ref, after_ref, *refs):
    del after_ref
    out_refs, window = refs[:SIDES], refs[SIDES]
    span, own = W * LEAF, LEAVES * LEAF
    window[:, :span] = left_ref[:, :span]
    window[:, span + own :] = right_ref[:, :span]
    for row, p in enumerate((p0, p1, p2, p3)):
        window[row * COLS : (row + 1) * COLS, span : span + own] = p[...]
    for pair in range(PAIRS):
        results = []
        for t in (2 * pair, 2 * pair + 1):
            sources = []
            for k in range(NEAR):
                start = pl.multiple_of((W + t + offset_ref[k, t]) * LEAF, LEAF)
                sources.append(window[:, pl.ds(start, LEAF)])
            results.append(near_leaf(sources, blocks_ref, t))
        store_pair(out_refs, pair, results)


def near_field(offsets, pieces, left, right, blocks, after):
    return pl.pallas_call(
        near_kernel,
        in_specs=[SMEM] + [VMEM] * 7 + [ANY],
        out_specs=[VMEM] * SIDES,
        out_shape=[like((PAIRS * COLS, 6 * RANK))] * SIDES,
        scratch_shapes=[pltpu.VMEM((SIDES * COLS, (LEAVES + 2 * W) * LEAF), BF16)],
        compiler_params=params(8),
        cost_estimate=cost(6 * 10**9, 2**22),
        name="near_field",
    )(offsets, *pieces, left, right, blocks, after)


def by_operator(flat):
    return jnp.concatenate([flat[:, o * RANK : (o + 1) * RANK] for o in range(OPS)], axis=0)


def half_of(children, odd):
    return jnp.where(odd == 1, children[:, RANK:], children[:, :RANK])


def couple_kernel(offset_ref, pairs_ref, left_ref, right_ref, coupling_ref, out_ref, near_coef):
    def spread(first, source):
        for i in range(source.shape[0] // COLS):
            both = source[i * COLS : (i + 1) * COLS, :]
            near_coef[first + 2 * i] = both[:, :RANK]
            near_coef[first + 2 * i + 1] = both[:, RANK:]

    spread(0, left_ref[:, W * LEAF :])
    spread(W, pairs_ref[...])
    spread(W + LEAVES, right_ref[:, W * LEAF :])
    for t in range(LEAVES):
        wide = jnp.concatenate([near_coef[W + t + offset_ref[k, t]] for k in range(FAR)], axis=1)
        out_ref[t] = by_operator(dot_nt(wide, coupling_ref[:, t].reshape(OPS * RANK, FAR * RANK)))


def couple_leaves(offsets, pairs, left, right, coupling):
    return pl.pallas_call(
        couple_kernel,
        in_specs=[SMEM] + [VMEM] * 4,
        out_specs=VMEM,
        out_shape=like((LEAVES, OPS * COLS, RANK), F32),
        scratch_shapes=[pltpu.VMEM((LEAVES + 2 * W, COLS, RANK), BF16)],
        compiler_params=params(8),
        cost_estimate=cost(3 * 10**9, 2**22),
        name="couple_leaves",
    )(offsets, pairs, left, right, coupling)


def far_kernel(
    where_ref,
    roots_ref,
    coupled_ref,
    root_ref,
    upper_hbm,
    top_ref,
    transfer_ref,
    basis_ref,
    out_ref,
    upper1,
    upper2,
    sems,
):
    q = where_ref[0]
    staged = Staged(
        [(upper_hbm.at[:, q >> 1], upper1), (upper_hbm.at[:, ROOTS // 2 + (q >> 2)], upper2)], sems, 2
    )

    def valid(c, height):
        return jnp.logical_and(c >= 0, c < (ROOTS >> height))

    def clip(c, height):
        return jnp.minimum(jnp.maximum(c, 0), (ROOTS >> height) - 1)

    def coef(height, c):
        if height == 0:
            return roots_ref[c - q + WINDOW // 2]
        first = (0, ROOTS // 2)[height - 1]
        joined = jnp.concatenate([coef(height - 1, 2 * c), coef(height - 1, 2 * c + 1)], axis=1)
        return dot_nt(joined, top_ref[first + c]).astype(BF16)

    def sources(height):
        c = q >> height
        odd = c % 2
        parts = []
        for even_step, odd_step in ((-2, -3), (2, -2), (3, 2)):
            other = c + jnp.where(odd == 1, odd_step, even_step)
            value = coef(height, clip(other, height))
            parts.append(jnp.where(valid(other, height), value, jnp.zeros_like(value)))
        return jnp.concatenate(parts, axis=1)

    wides = [sources(height) for height in range(TOPL)]
    staged.wait(1)
    couplings = [root_ref[:, 0], upper1[...], upper2[...]]
    fields = [
        dot_nt(wide, coupling.reshape(OPS * RANK, 3 * RANK))
        for wide, coupling in zip(wides, couplings)
    ]
    running = by_operator(fields[2])
    children = dot_nn(running.astype(BF16), top_ref[ROOTS // 2 + (q >> 2)])
    running = by_operator(fields[1]) + half_of(children, (q >> 1) % 2)
    children = dot_nn(running.astype(BF16), top_ref[q >> 1])
    running = by_operator(fields[0]) + half_of(children, q % 2)

    level = [running]
    last = LEAVES - 1
    while len(level) < LEAVES:
        count = len(level)
        last -= count
        lower = []
        for i, value in enumerate(level):
            children = dot_nn(value.astype(BF16), transfer_ref[last + i])
            lower += [children[:, :RANK], children[:, RANK:]]
        level = lower

    for t in range(LEAVES):
        far = dot_nn((level[t] + coupled_ref[t]).astype(BF16), basis_ref[t])
        out_ref[:, :, t * LEAF : (t + 1) * LEAF] = far.reshape(OPS, COLS, LEAF)


def far_field(where, roots, coupled, root_coupling, upper, top, transfer, basis):
    return pl.pallas_call(
        far_kernel,
        in_specs=[SMEM] + [VMEM] * 3 + [HBM] + [VMEM] * 3,
        out_specs=VMEM,
        out_shape=like((OPS, COLS, LEAVES * LEAF), F32),
        scratch_shapes=[
            pltpu.VMEM((OPS, RANK, 3 * RANK), BF16),
            pltpu.VMEM((OPS, RANK, 3 * RANK), BF16),
            pltpu.SemaphoreType.DMA((2,)),
        ],
        compiler_params=params(8),
        cost_estimate=cost(3 * 10**9, 2**22),
        name="far_field",
    )(where, roots, coupled, root_coupling, in_hbm(upper), top, transfer, basis)


def join_kernel(where_ref, far_ref, n0, n1, n2, n3, out_ref, ordered):
    me = where_ref[0]
    for step, near in enumerate((n0, n1, n2, n3)):
        ordered[lax.rem(me + SIDES - step, SIDES)] = near[...]
    for pair in range(PAIRS):
        parts = [ordered[r, pair * COLS : (pair + 1) * COLS].astype(F32) for r in range(SIDES)]
        for e in (0, 1):
            for o in range(OPS):
                at = (e * OPS + o) * RANK
                near = jnp.concatenate([part[:, at : at + RANK] for part in parts], axis=1)
                columns = slice((2 * pair + e) * LEAF, (2 * pair + e + 1) * LEAF)
                out_ref[o, :, columns] = (far_ref[o, :, columns] + near).astype(BF16)


def join(where, far, near):
    return pl.pallas_call(
        join_kernel,
        in_specs=[SMEM] + [VMEM] * (1 + SIDES),
        out_specs=VMEM,
        out_shape=jax.ShapeDtypeStruct((OPS, COLS, LEAVES * LEAF), BF16),
        scratch_shapes=[pltpu.VMEM((SIDES, PAIRS * COLS, 6 * RANK), BF16)],
        compiler_params=params(8),
        cost_estimate=cost(2**20, 2**22),
        name="join",
    )(where, far, *near)


def round_rhs(value, step):
    return lax.ppermute(value, "rhs", [(i, (i + step) % SIDES) for i in range(SIDES)])


def round_leaf(value, step):
    count = lax.axis_size("leaf")
    return lax.ppermute(value, "leaf", [(i, (i + step) % count) for i in range(count)])


def along_leaf(value, step):
    count = lax.axis_size("leaf")
    return lax.ppermute(
        value, "leaf", [(i, i + step) for i in range(count) if 0 <= i + step < count]
    )


def per_device(
    points,
    leaf_basis,
    local_transfer,
    top_transfer,
    leaf_coupling,
    root_coupling,
    upper_coupling,
    near_blocks,
    near_offset,
    far_offset,
):
    leaf_index = lax.axis_index("leaf").astype(jnp.int32).reshape(1)
    rhs_index = lax.axis_index("rhs").astype(jnp.int32).reshape(1)

    def grow(roots, after=None):
        more = round_leaf(roots, -roots.shape[0])
        return append(roots, more, roots if after is None else after)

    transfer = local_transfer[0]
    pieces = [points] + [round_rhs(points, -step) for step in range(1, SIDES)]
    pairs, root = upsweep(points, leaf_basis, transfer)
    roots = grow(grow(root))
    head, tail = pack_halos(pieces, pairs, roots)
    left = along_leaf(tail, 1)
    right = along_leaf(head, -1)
    near = near_field(near_offset.T, pieces, left, right, near_blocks, roots)
    roots = grow(roots, near[0])
    roots = grow(roots)
    near = [near[0]] + [round_rhs(near[step], step) for step in range(1, SIDES)]
    coupled = couple_leaves(far_offset.T, pairs, left, right, leaf_coupling)
    roots = append(round_leaf(roots, WINDOW // 2), roots, coupled)
    far = far_field(
        leaf_index, roots, coupled, root_coupling, upper_coupling, top_transfer, transfer, leaf_basis
    )
    return join(rhs_index, far, near)


def solution(mesh):
    placed = (
        P("rhs", "leaf"),
        P("leaf", None, None),
        P("leaf", None, None, None),
        P(),
        P(None, "leaf", None, None),
        P(None, "leaf", None, None),
        P(),
        P(None, "leaf", None, "rhs", None),
        P("leaf", None),
        P("leaf", None),
    )
    return jax.shard_map(
        per_device, mesh=mesh, in_specs=placed, out_specs=P(None, "rhs", "leaf"), check_vma=False
    )
```

time: 80.9 us -> 55.2 us (0.68)
  the two profiles are of different devices: /device:TPU:8 before, /device:TPU:89 now
where the time goes in v2:
time: 55.2 us; the launch traced here: 55 us
  starting transfers between devices  20.1 us (36%)
  waiting for transfers between devices  18.1 us (33%)
  Pallas kernels  14.2 us (26%)
  local copies, waits for them, and re-layouts  2.38 us (4%)
    ppermute x5, waiting for transfers between devices, round_leaf(): lax.ppermute(value, 'leaf', [(i, (i + step) % count) for i in range(count)])  10.7 us
    ppermute x6, starting transfers between devices, round_rhs(): lax.ppermute(value, 'rhs', [(i, (i + step) % SIDES) for i in range(SIDES)])  9.22 us
    ppermute x2, waiting for transfers between devices, along_leaf(): lax.ppermute(value, 'leaf', [(i, i + step) for i in range(count) if 0 <=...  7.4 us
    ppermute x5, starting transfers between devices, round_leaf(): lax.ppermute(value, 'leaf', [(i, (i + step) % count) for i in range(count)])  6.38 us
    ppermute x2, starting transfers between devices, along_leaf(): lax.ppermute(value, 'leaf', [(i, i + step) for i in range(count) if 0 <=...  4.46 us
    pallas_call x1, Pallas kernels, near_field(): pl.pallas_call(near_kernel, in_specs=[SMEM] + [VMEM] * 7 + [ANY], out_spe...  3.86 us
    pallas_call x1, Pallas kernels, far_field(): pl.pallas_call(far_kernel, in_specs=[SMEM] + [VMEM] * 3 + [HBM] + [VMEM]...  3.33 us
    pallas_call x1, Pallas kernels, upsweep(): pl.pallas_call(up_kernel, in_specs=[HBM] * 3, out_specs=[VMEM] * 2, out_s...  2.94 us
  transfers between devices with their start and end apart: 13, of which 5 were waited for; matrix products, arithmetic and copies ran while one was open for 0% of the time, Pallas kernels for 23%

profile of v2, /device:TPU:89, one launch (start us, length us, event | category | flops | bytes accessed | tf_op | source)
XLA Modules:
  0.0 55.0 jit_solution(1224697919033287163)
XLA Ops:
  0.0 1.2 %collective-permute-start.5 = (bf16[16,8192]{1,0:T(8,128)(2,1)}, bf16[16,8192]{1,0:T(8,128)(2,1)S(1)}, u32[]{:S(2)}, u32[]{:S(2)}) collective-permute-start(bf16[16,8192]{1,0:T(8,128)(2,1)} %p0.3), channel_id=1, source_target_pairs={{0,1},{1,2},{2,3},{3,0},{4,5},{5,6},{6,7},{7,4},{8,9},{9,10},{10,1... | collective-permute-start | bytes 786440 | tf_op jit(solution)/shard_map/ppermute | solution.py:373
  1.2 2.5 %collective-permute-start.4 = (bf16[16,8192]{1,0:T(8,128)(2,1)}, bf16[16,8192]{1,0:T(8,128)(2,1)S(1)}, u32[]{:S(2)}, u32[]{:S(2)}) collective-permute-start(bf16[16,8192]{1,0:T(8,128)(2,1)} %p0.3), channel_id=1, source_target_pairs={{0,2},{1,3},{2,0},{3,1},{4,6},{5,7},{6,4},{7,5},{8,10},{9,11},{10,... | collective-permute-start | bytes 786440 | tf_op jit(solution)/shard_map/ppermute | solution.py:373
  3.7 1.2 %collective-permute-start.3 = (bf16[16,8192]{1,0:T(8,128)(2,1)}, bf16[16,8192]{1,0:T(8,128)(2,1)S(1)}, u32[]{:S(2)}, u32[]{:S(2)}) collective-permute-start(bf16[16,8192]{1,0:T(8,128)(2,1)} %p0.3), channel_id=1, source_target_pairs={{0,3},{1,0},{2,1},{3,2},{4,7},{5,4},{6,5},{7,6},{8,11},{9,8},{10,9... | collective-permute-start | bytes 786440 | tf_op jit(solution)/shard_map/ppermute | solution.py:373
  4.8 0.0 copy-start.4
  4.8 0.0 slice-start
  4.8 0.0 slice-start.1
  4.8 2.9 %upsweep.1 = (bf16[256,128]{1,0:T(8,128)(2,1)S(1)}, bf16[1,16,64]{2,1,0:T(8,128)(2,1)S(1)}) custom-call(bf16[16,8192]{1,0:T(8,128)(2,1)} %p0.3, bf16[32,64,256]{2,1,0:T(8,128)(2,1)} %basis_ref.1, bf16[31,64,128]{2,1,0:T(8,128)(2,1)} %bitcast.7), custom_call_target="tpu_custom_call" | custom-call | flops 8589934592 | bytes 1048576 | tf_op jit(solution)/shard_map/upsweep/pallas_call | solution.py:115
  7.8 1.6 %collective-permute-start = (bf16[1,16,64]{2,1,0:T(8,128)(2,1)S(1)}, bf16[1,16,64]{2,1,0:T(8,128)(2,1)S(1)}, u32[]{:S(2)}, u32[]{:S(2)}) collective-permute-start(bf16[1,16,64]{2,1,0:T(8,128)(2,1)S(1)} %get-tuple-element.13.first_ref.after_ref), channel_id=1, source_target_pairs={{0,252},{4,0},{8,4},{12,8},{16,12},{20,16},{24,20},{28,24},{32,28}... | collective-permute-start | bytes 6152 | tf_op jit(solution)/shard_map/ppermute | solution.py:378
  9.4 3.9 %collective-permute-done.second_ref = bf16[1,16,64]{2,1,0:T(8,128)(2,1)S(1)} collective-permute-done((bf16[1,16,64]{2,1,0:T(8,128)(2,1)S(1)}, bf16[1,16,64]{2,1,0:T(8,128)(2,1)S(1)}, u32[]{:S(2)}, u32[]{:S(2)}) %collective-permute-start) | collective-permute-done | bytes 2080 | tf_op jit(solution)/shard_map/ppermute | solution.py:378
  13.3 0.0 collective-permute-start.1
  13.3 4.6 %collective-permute-done.1.second_ref = bf16[2,16,64]{2,1,0:T(8,128)(2,1)S(1)} collective-permute-done((bf16[2,16,64]{2,1,0:T(8,128)(2,1)S(1)}, bf16[2,16,64]{2,1,0:T(8,128)(2,1)S(1)}, u32[]{:S(2)}, u32[]{:S(2)}) %collective-permute-start.1) | collective-permute-done | bytes 4128 | tf_op jit(solution)/shard_map/ppermute | solution.py:378
  17.9 0.0 collective-permute-done.5.p3
  17.9 0.0 collective-permute-done.4.p2
  17.9 0.0 collective-permute-done.3.p1
  17.9 0.0 copy-done.4
  17.9 0.0 slice-start.2
  18.0 0.0 copy-start.7
  18.0 2.1 %collective-permute-start.6 = (bf16[64,2176]{1,0:T(8,128)(2,1)S(1)}, bf16[64,2176]{1,0:T(8,128)(2,1)S(1)}, u32[]{:S(2)}, u32[]{:S(2)}) collective-permute-start(bf16[64,2176]{1,0:T(8,128)(2,1)S(1)} %get-tuple-element.15), channel_id=1, source_target_pairs={{0,4},{4,8},{8,12},{12,16},{16,20},{20,24},{24,28},{28,32},{32,36}... | collective-permute-start | bytes 835592 | tf_op jit(solution)/shard_map/ppermute | solution.py:383
  20.1 2.4 %collective-permute-start.7 = (bf16[64,2176]{1,0:T(8,128)(2,1)S(1)}, bf16[64,2176]{1,0:T(8,128)(2,1)S(1)}, u32[]{:S(2)}, u32[]{:S(2)}) collective-permute-start(bf16[64,2176]{1,0:T(8,128)(2,1)S(1)} %get-tuple-element.16), channel_id=1, source_target_pairs={{4,0},{8,4},{12,8},{16,12},{20,16},{24,20},{28,24},{32,28},{36,32}... | collective-permute-start | bytes 835592 | tf_op jit(solution)/shard_map/ppermute | solution.py:383
  22.5 0.5 collective-permute-start.2
  23.0 0.5 collective-permute-done.6.left_ref
  23.6 6.9 %collective-permute-done.7.right_ref = bf16[64,2176]{1,0:T(8,128)(2,1)S(1)} collective-permute-done((bf16[64,2176]{1,0:T(8,128)(2,1)S(1)}, bf16[64,2176]{1,0:T(8,128)(2,1)S(1)}, u32[]{:S(2)}, u32[]{:S(2)}) %collective-permute-start.7) | collective-permute-done | bytes 278560 | tf_op jit(solution)/shard_map/ppermute | solution.py:383
  30.4 0.0 slice-done
  30.4 0.0 slice-done.1
  30.4 0.0 slice-done.2
  30.4 0.0 copy-done.7
  30.4 0.0 copy-start.6
  30.5 3.9 %near_field.1 = (bf16[256,384]{1,0:T(8,128)(2,1)S(1)}, bf16[256,384]{1,0:T(8,128)(2,1)S(1)}, bf16[256,384]{1,0:T(8,128)(2,1)S(1)}, bf16[256,384]{1,0:T(8,128)(2,1)S(1)}) custom-call(s32[3,32]{1,0:T(4,128)S(1)} %bitcast.10, bf16[16,8192]{1,0:T(8,128)(2,1)S(1)} %copy-done.4, bf16[16,8192]{1,0:T(8,128)(2,1)S(1)} %collective-permute-done.3.p1, ...), custom_call_target="tpu_custom_call" | custom-call | flops 6000000000 | bytes 4194304 | tf_op jit(solution)/shard_map/near_field/pallas_call | solution.py:209
  34.3 0.0 collective-permute-done.2.second_ref
  34.3 0.1 collective-permute-start.8
  34.4 1.0 %collective-permute-start.10 = (bf16[256,384]{1,0:T(8,128)(2,1)S(1)}, bf16[256,384]{1,0:T(8,128)(2,1)S(1)}, u32[]{:S(2)}, u32[]{:S(2)}) collective-permute-start(bf16[256,384]{1,0:T(8,128)(2,1)S(1)} %get-tuple-element.18), channel_id=1, source_target_pairs={{0,1},{1,2},{2,3},{3,0},{4,5},{5,6},{6,7},{7,4},{8,9},{9,10},{10,1... | collective-permute-start | bytes 589832 | tf_op jit(solution)/shard_map/ppermute | solution.py:373
  35.5 2.1 %collective-permute-start.11 = (bf16[256,384]{1,0:T(8,128)(2,1)S(1)}, bf16[256,384]{1,0:T(8,128)(2,1)S(1)}, u32[]{:S(2)}, u32[]{:S(2)}) collective-permute-start(bf16[256,384]{1,0:T(8,128)(2,1)S(1)} %get-tuple-element.19), channel_id=1, source_target_pairs={{0,2},{1,3},{2,0},{3,1},{4,6},{5,7},{6,4},{7,5},{8,10},{9,11},{10,... | collective-permute-start | bytes 589832 | tf_op jit(solution)/shard_map/ppermute | solution.py:373
  37.6 1.3 %collective-permute-start.12 = (bf16[256,384]{1,0:T(8,128)(2,1)S(1)}, bf16[256,384]{1,0:T(8,128)(2,1)S(1)}, u32[]{:S(2)}, u32[]{:S(2)}) collective-permute-start(bf16[256,384]{1,0:T(8,128)(2,1)S(1)} %get-tuple-element.20), channel_id=1, source_target_pairs={{0,3},{1,0},{2,1},{3,2},{4,7},{5,4},{6,5},{7,6},{8,11},{9,8},{10,9... | collective-permute-start | bytes 589832 | tf_op jit(solution)/shard_map/ppermute | solution.py:373
  38.8 2.2 %collective-permute-done.8.second_ref = bf16[8,16,64]{2,1,0:T(8,128)(2,1)S(1)} collective-permute-done((bf16[8,16,64]{2,1,0:T(8,128)(2,1)S(1)}, bf16[8,16,64]{2,1,0:T(8,128)(2,1)S(1)}, u32[]{:S(2)}, u32[]{:S(2)}) %collective-permute-start.8) | collective-permute-done | bytes 16416 | tf_op jit(solution)/shard_map/ppermute | solution.py:378
  41.0 4.2 %collective-permute-start.9 = (bf16[16,16,64]{2,1,0:T(8,128)(2,1)S(1)}, bf16[16,16,64]{2,1,0:T(8,128)(2,1)S(1)}, u32[]{:S(2)}, u32[]{:S(2)}) collective-permute-start(bf16[16,16,64]{2,1,0:T(8,128)(2,1)S(1)} %append.8.second_ref), channel_id=1, source_target_pairs={{0,64},{4,68},{8,72},{12,76},{16,80},{20,84},{24,88},{28,92},{32,9... | collective-permute-start | bytes 98312 | tf_op jit(solution)/shard_map/ppermute | solution.py:378
  45.2 0.0 copy-done.6
  45.2 0.0 copy-start
  45.2 2.3 %copy-done = bf16[3,32,64,320]{3,2,1,0:T(8,128)(2,1)S(1)} copy-done((bf16[3,32,64,320]{3,2,1,0:T(8,128)(2,1)S(1)}, bf16[3,32,64,320]{3,2,1,0:T(8,128)(2,1)}, u32[]{:S(2)}) %copy-start) | copy-done | bytes 3932184
  47.6 0.0 copy-start.1
  47.6 0.0 copy-start.2
  47.6 0.0 copy-start.3
  47.6 0.0 copy-start.5
  47.6 2.6 %couple_leaves.1.after_ref.coupled_ref = f32[32,48,64]{2,1,0:T(8,128)S(1)} custom-call(s32[5,32]{1,0:T(8,128)S(1)} %bitcast.9, bf16[256,128]{1,0:T(8,128)(2,1)S(1)} %get-tuple-element.14.pairs_ref, bf16[64,2176]{1,0:T(8,128)(2,1)S(1)} %collective-permute-done.6.left_ref, bf16[64,2176]{1,0:T(8,128)(2,1)S(1)} %collective-permute-done.7.right_ref, ...), custom_call_target="tpu_custom_call" | custom-call | flops 3000000000 | bytes 4194304 | tf_op jit(solution)/shard_map/couple_leaves/pallas_call | solution.py:245
  50.1 0.0 collective-permute-done.9.first_ref
  50.2 0.0 copy-done.1
  50.2 0.0 copy-done.2
  50.2 0.0 copy-done.3
  50.2 0.0 copy-done.5
  50.2 3.3 %far_field.1.far_ref = f32[3,16,8192]{2,1,0:T(8,128)S(1)} custom-call(s32[1]{0:T(128)} %bitcast.1.where_ref, bf16[32,16,64]{2,1,0:T(8,128)(2,1)S(1)} %append.9.roots_ref, f32[32,48,64]{2,1,0:T(8,128)S(1)} %couple_leaves.1.after_ref.coupled_ref, bf16[3,1,64,192]{3,2,1,0:T(8,128)(2,1)S(1)} %copy-done.5, bf16[3,48,64,192]{3,2,1,0:T(8,128)(2,1)} %upper_hbm.1, ...), custom_call_target="tpu_custom_call" | custom-call | flops 3000000000 | bytes 4194304 | tf_op jit(solution)/shard_map/far_field/pallas_call | solution.py:329
  53.6 0.0 collective-permute-done.10.n1
  53.6 0.0 collective-permute-done.11.n2
  53.6 0.0 collective-permute-done.12.n3
  53.6 1.4 %join.1 = bf16[3,16,8192]{2,1,0:T(8,128)(2,1)} custom-call(s32[1]{0:T(128)} %bitcast.where_ref, f32[3,16,8192]{2,1,0:T(8,128)S(1)} %far_field.1.far_ref, bf16[256,384]{1,0:T(8,128)(2,1)S(1)} %get-tuple-element.17.after_ref.n0, bf16[256,384]{1,0:T(8,128)(2,1)S(1)} %collective-permute-done.10.n1, bf16[256,384]{1,0:T(8,128)(2,1)S(1)} %collective-permute-done.11.n2, ...), custom_call_target="tpu_custom_call" | custom-call | flops 1048576 | bytes 4194304 | tf_op jit(solution)/shard_map/join/pallas_call | solution.py:360
  (7 shorter events, 0.1 us)
Async XLA Ops:
  0.0 17.9 %collective-permute-start.5 = (bf16[16,8192]{1,0:T(8,128)(2,1)}, bf16[16,8192]{1,0:T(8,128)(2,1)S(1)}, u32[]{:S(2)}, u32[]{:S(2)}) collective-permute-start(bf16[16,8192]{1,0:T(8,128)(2,1)} %p0.3), channel_id=1, source_target_pairs={{0,1},{1,2},{2,3},{3,0},{4,5},{5,6},{6,7},{7,4},{8,9},{9,10},{10,1... | collective-permute-start | bytes 786440 | tf_op jit(solution)/shard_map/ppermute | solution.py:373
  1.2 16.7 %collective-permute-start.4 = (bf16[16,8192]{1,0:T(8,128)(2,1)}, bf16[16,8192]{1,0:T(8,128)(2,1)S(1)}, u32[]{:S(2)}, u32[]{:S(2)}) collective-permute-start(bf16[16,8192]{1,0:T(8,128)(2,1)} %p0.3), channel_id=1, source_target_pairs={{0,2},{1,3},{2,0},{3,1},{4,6},{5,7},{6,4},{7,5},{8,10},{9,11},{10,... | collective-permute-start | bytes 786440 | tf_op jit(solution)/shard_map/ppermute | solution.py:373
  3.7 14.3 %collective-permute-start.3 = (bf16[16,8192]{1,0:T(8,128)(2,1)}, bf16[16,8192]{1,0:T(8,128)(2,1)S(1)}, u32[]{:S(2)}, u32[]{:S(2)}) collective-permute-start(bf16[16,8192]{1,0:T(8,128)(2,1)} %p0.3), channel_id=1, source_target_pairs={{0,3},{1,0},{2,1},{3,2},{4,7},{5,4},{6,5},{7,6},{8,11},{9,8},{10,9... | collective-permute-start | bytes 786440 | tf_op jit(solution)/shard_map/ppermute | solution.py:373
  4.8 13.1 %copy-start.4 = (bf16[16,8192]{1,0:T(8,128)(2,1)S(1)}, bf16[16,8192]{1,0:T(8,128)(2,1)}, u32[]{:S(2)}) copy-start(bf16[16,8192]{1,0:T(8,128)(2,1)} %p0.3) | copy-start | bytes 786436
  4.8 25.6 %slice-start = ((s8[9437184]{0:T(1024)(128)(4,1)}), s8[4194304]{0:T(1024)(128)(4,1)S(1)}, s32[]{:S(2)}) async-start(s8[9437184]{0:T(1024)(128)(4,1)} %bitcast.5), calls=%async_computation | async-start | bytes 8388608
  4.8 25.6 %slice-start.1 = ((s8[9437184]{0:T(1024)(128)(4,1)}), s8[4194304]{0:T(1024)(128)(4,1)S(1)}, s32[]{:S(2)}) async-start(s8[9437184]{0:T(1024)(128)(4,1)} %bitcast.5), calls=%async_computation.1 | async-start | bytes 8388608
  7.8 5.5 %collective-permute-start = (bf16[1,16,64]{2,1,0:T(8,128)(2,1)S(1)}, bf16[1,16,64]{2,1,0:T(8,128)(2,1)S(1)}, u32[]{:S(2)}, u32[]{:S(2)}) collective-permute-start(bf16[1,16,64]{2,1,0:T(8,128)(2,1)S(1)} %get-tuple-element.13.first_ref.after_ref), channel_id=1, source_target_pairs={{0,252},{4,0},{8,4},{12,8},{16,12},{20,16},{24,20},{28,24},{32,28}... | collective-permute-start | bytes 6152 | tf_op jit(solution)/shard_map/ppermute | solution.py:378
  13.3 4.6 %collective-permute-start.1 = (bf16[2,16,64]{2,1,0:T(8,128)(2,1)S(1)}, bf16[2,16,64]{2,1,0:T(8,128)(2,1)S(1)}, u32[]{:S(2)}, u32[]{:S(2)}) collective-permute-start(bf16[2,16,64]{2,1,0:T(8,128)(2,1)S(1)} %append.5.first_ref.after_ref), channel_id=1, source_target_pairs={{0,248},{4,252},{8,0},{12,4},{16,8},{20,12},{24,16},{28,20},{32,24... | collective-permute-start | bytes 12296 | tf_op jit(solution)/shard_map/ppermute | solution.py:378
  17.9 12.5 %slice-start.2 = ((s8[9437184]{0:T(1024)(128)(4,1)}), s8[1048576]{0:T(1024)(128)(4,1)S(1)}, s32[]{:S(2)}) async-start(s8[9437184]{0:T(1024)(128)(4,1)} %bitcast.5), calls=%async_computation.2 | async-start | bytes 2097152
  18.0 12.5 %copy-start.7 = (s32[32,3]{0,1:T(4,128)S(1)}, s32[32,3]{0,1:T(4,128)}, u32[]{:S(2)}) copy-start(s32[32,3]{0,1:T(4,128)} %param.18) | copy-start | bytes 1156
  18.0 5.5 %collective-permute-start.6 = (bf16[64,2176]{1,0:T(8,128)(2,1)S(1)}, bf16[64,2176]{1,0:T(8,128)(2,1)S(1)}, u32[]{:S(2)}, u32[]{:S(2)}) collective-permute-start(bf16[64,2176]{1,0:T(8,128)(2,1)S(1)} %get-tuple-element.15), channel_id=1, source_target_pairs={{0,4},{4,8},{8,12},{12,16},{16,20},{20,24},{24,28},{28,32},{32,36}... | collective-permute-start | bytes 835592 | tf_op jit(solution)/shard_map/ppermute | solution.py:383
  20.1 10.3 %collective-permute-start.7 = (bf16[64,2176]{1,0:T(8,128)(2,1)S(1)}, bf16[64,2176]{1,0:T(8,128)(2,1)S(1)}, u32[]{:S(2)}, u32[]{:S(2)}) collective-permute-start(bf16[64,2176]{1,0:T(8,128)(2,1)S(1)} %get-tuple-element.16), channel_id=1, source_target_pairs={{4,0},{8,4},{12,8},{16,12},{20,16},{24,20},{28,24},{32,28},{36,32}... | collective-permute-start | bytes 835592 | tf_op jit(solution)/shard_map/ppermute | solution.py:383
  22.5 11.8 %collective-permute-start.2 = (bf16[4,16,64]{2,1,0:T(8,128)(2,1)S(1)}, bf16[4,16,64]{2,1,0:T(8,128)(2,1)S(1)}, u32[]{:S(2)}, u32[]{:S(2)}) collective-permute-start(bf16[4,16,64]{2,1,0:T(8,128)(2,1)S(1)} %append.6.after_ref.first_ref), channel_id=1, source_target_pairs={{0,240},{4,244},{8,248},{12,252},{16,0},{20,4},{24,8},{28,12},{32,... | collective-permute-start | bytes 24584 | tf_op jit(solution)/shard_map/ppermute | solution.py:378
  30.4 14.8 %copy-start.6 = (s32[32,5]{0,1:T(8,128)S(1)}, s32[32,5]{0,1:T(8,128)}, u32[]{:S(2)}) copy-start(s32[32,5]{0,1:T(8,128)} %param.19) | copy-start | bytes 1924
  34.3 6.7 %collective-permute-start.8 = (bf16[8,16,64]{2,1,0:T(8,128)(2,1)S(1)}, bf16[8,16,64]{2,1,0:T(8,128)(2,1)S(1)}, u32[]{:S(2)}, u32[]{:S(2)}) collective-permute-start(bf16[8,16,64]{2,1,0:T(8,128)(2,1)S(1)} %append.7.first_ref.after_ref), channel_id=1, source_target_pairs={{0,224},{4,228},{8,232},{12,236},{16,240},{20,244},{24,248},{28,25... | collective-permute-start | bytes 49160 | tf_op jit(solution)/shard_map/ppermute | solution.py:378
  34.4 19.1 %collective-permute-start.10 = (bf16[256,384]{1,0:T(8,128)(2,1)S(1)}, bf16[256,384]{1,0:T(8,128)(2,1)S(1)}, u32[]{:S(2)}, u32[]{:S(2)}) collective-permute-start(bf16[256,384]{1,0:T(8,128)(2,1)S(1)} %get-tuple-element.18), channel_id=1, source_target_pairs={{0,1},{1,2},{2,3},{3,0},{4,5},{5,6},{6,7},{7,4},{8,9},{9,10},{10,1... | collective-permute-start | bytes 589832 | tf_op jit(solution)/shard_map/ppermute | solution.py:373
  35.5 18.1 %collective-permute-start.11 = (bf16[256,384]{1,0:T(8,128)(2,1)S(1)}, bf16[256,384]{1,0:T(8,128)(2,1)S(1)}, u32[]{:S(2)}, u32[]{:S(2)}) collective-permute-start(bf16[256,384]{1,0:T(8,128)(2,1)S(1)} %get-tuple-element.19), channel_id=1, source_target_pairs={{0,2},{1,3},{2,0},{3,1},{4,6},{5,7},{6,4},{7,5},{8,10},{9,11},{10,... | collective-permute-start | bytes 589832 | tf_op jit(solution)/shard_map/ppermute | solution.py:373
  37.6 16.0 %collective-permute-start.12 = (bf16[256,384]{1,0:T(8,128)(2,1)S(1)}, bf16[256,384]{1,0:T(8,128)(2,1)S(1)}, u32[]{:S(2)}, u32[]{:S(2)}) collective-permute-start(bf16[256,384]{1,0:T(8,128)(2,1)S(1)} %get-tuple-element.20), channel_id=1, source_target_pairs={{0,3},{1,0},{2,1},{3,2},{4,7},{5,4},{6,5},{7,6},{8,11},{9,8},{10,9... | collective-permute-start | bytes 589832 | tf_op jit(solution)/shard_map/ppermute | solution.py:373
  41.0 9.1 %collective-permute-start.9 = (bf16[16,16,64]{2,1,0:T(8,128)(2,1)S(1)}, bf16[16,16,64]{2,1,0:T(8,128)(2,1)S(1)}, u32[]{:S(2)}, u32[]{:S(2)}) collective-permute-start(bf16[16,16,64]{2,1,0:T(8,128)(2,1)S(1)} %append.8.second_ref), channel_id=1, source_target_pairs={{0,64},{4,68},{8,72},{12,76},{16,80},{20,84},{24,88},{28,92},{32,9... | collective-permute-start | bytes 98312 | tf_op jit(solution)/shard_map/ppermute | solution.py:378
  45.2 2.3 %copy-start = (bf16[3,32,64,320]{3,2,1,0:T(8,128)(2,1)S(1)}, bf16[3,32,64,320]{3,2,1,0:T(8,128)(2,1)}, u32[]{:S(2)}) copy-start(bf16[3,32,64,320]{3,2,1,0:T(8,128)(2,1)} %coupling_ref.1) | copy-start | bytes 11796484
  47.6 2.6 %copy-start.1 = (bf16[32,64,256]{2,1,0:T(8,128)(2,1)S(1)}, bf16[32,64,256]{2,1,0:T(8,128)(2,1)}, u32[]{:S(2)}) copy-start(bf16[32,64,256]{2,1,0:T(8,128)(2,1)} %basis_ref.1) | copy-start | bytes 3145732
  47.6 2.6 %copy-start.2 = (bf16[48,64,128]{2,1,0:T(8,128)(2,1)S(1)}, bf16[48,64,128]{2,1,0:T(8,128)(2,1)}, u32[]{:S(2)}) copy-start(bf16[48,64,128]{2,1,0:T(8,128)(2,1)} %top_ref.1) | copy-start | bytes 2359300
  47.6 2.7 %copy-start.3 = (bf16[1,31,64,128]{3,2,1,0:T(8,128)(2,1)S(1)}, bf16[1,31,64,128]{3,2,1,0:T(8,128)(2,1)}, u32[]{:S(2)}) copy-start(bf16[1,31,64,128]{3,2,1,0:T(8,128)(2,1)} %param.12) | copy-start | bytes 1523716
  47.6 2.7 %copy-start.5 = (bf16[3,1,64,192]{3,2,1,0:T(8,128)(2,1)S(1)}, bf16[3,1,64,192]{3,2,1,0:T(8,128)(2,1)}, u32[]{:S(2)}) copy-start(bf16[3,1,64,192]{3,2,1,0:T(8,128)(2,1)} %root_ref.1) | copy-start | bytes 221188

commit v3 on v2

--- a/solution.py
+++ b/solution.py
@@ -148,7 +148,7 @@
         out_specs=[VMEM] * 2,
         out_shape=[like((SIDES * COLS, HALO))] * 2,
         compiler_params=params(4),
-        cost_estimate=cost(2**33, 2**20),
+        cost_estimate=cost(0, 0),
         name="pack_halos",
     )(*pieces, pairs, after)
 
@@ -160,14 +160,14 @@
     out_ref[count:] = second_ref[...]
 
 
-def append(first, second, after):
+def append(first, second, after, weight=0):
     return pl.pallas_call(
         append_kernel,
         in_specs=[VMEM] * 2 + [ANY],
         out_specs=VMEM,
         out_shape=like((2 * first.shape[0], COLS, RANK)),
         compiler_params=params(4),
-        cost_estimate=cost(0, 0),
+        cost_estimate=cost(weight, 0),
         name="append",
     )(first, second, after)
 
@@ -400,20 +400,20 @@
     leaf_index = lax.axis_index("leaf").astype(jnp.int32).reshape(1)
     rhs_index = lax.axis_index("rhs").astype(jnp.int32).reshape(1)
 
-    def grow(roots, after=None):
+    def grow(roots, after=None, weight=0):
         more = round_leaf(roots, -roots.shape[0])
-        return append(roots, more, roots if after is None else after)
+        return append(roots, more, roots if after is None else after, weight)
 
     transfer = local_transfer[0]
     pieces = [points] + [round_rhs(points, -step) for step in range(1, SIDES)]
     pairs, root = upsweep(points, leaf_basis, transfer)
     roots = grow(grow(root))
-    head, tail = pack_halos(pieces, pairs, roots)
+    head, tail = pack_halos(pieces, pairs, root)
     left = along_leaf(tail, 1)
     right = along_leaf(head, -1)
     near = near_field(near_offset.T, pieces, left, right, near_blocks, roots)
+    roots = grow(roots, None, 2**33)
     roots = grow(roots, near[0])
-    roots = grow(roots)
     near = [near[0]] + [round_rhs(near[step], step) for step in range(1, SIDES)]
     coupled = couple_leaves(far_offset.T, pairs, left, right, leaf_coupling)
     roots = append(round_leaf(roots, WINDOW // 2), roots, coupled)

time: 55.2 us -> 55.5 us (level)
  the two profiles are of different devices: /device:TPU:89 before, /device:TPU:8 now
where the time goes in v3:
time: 55.5 us; the launch traced here: 54.9 us
  starting transfers between devices  29.6 us (53%)
  Pallas kernels  14.1 us (25%)
  waiting for transfers between devices  10.9 us (20%)
    ppermute x5, starting transfers between devices, round_leaf(): lax.ppermute(value, 'leaf', [(i, (i + step) % count) for i in range(count)])  13.4 us
    ppermute x6, starting transfers between devices, round_rhs(): lax.ppermute(value, 'rhs', [(i, (i + step) % SIDES) for i in range(SIDES)])  9.1 us
    ppermute x2, starting transfers between devices, along_leaf(): lax.ppermute(value, 'leaf', [(i, i + step) for i in range(count) if 0 <=...  7.07 us
    ppermute x6, waiting for transfers between devices, round_rhs(): lax.ppermute(value, 'rhs', [(i, (i + step) % SIDES) for i in range(SIDES)])  3.96 us
    ppermute x2, waiting for transfers between devices, along_leaf(): lax.ppermute(value, 'leaf', [(i, i + step) for i in range(count) if 0 <=...  3.93 us
    pallas_call x1, Pallas kernels, near_field(): pl.pallas_call(near_kernel, in_specs=[SMEM] + [VMEM] * 7 + [ANY], out_spe...  3.87 us
    pallas_call x1, Pallas kernels, far_field(): pl.pallas_call(far_kernel, in_specs=[SMEM] + [VMEM] * 3 + [HBM] + [VMEM]...  3.33 us
    ppermute x5, waiting for transfers between devices, round_leaf(): lax.ppermute(value, 'leaf', [(i, (i + step) % count) for i in range(count)])  2.98 us
  transfers between devices with their start and end apart: 13, of which 7 were waited for; matrix products, arithmetic and copies ran while one was open for 0% of the time, Pallas kernels for 23%

profile of v3, /device:TPU:8, one launch (start us, length us, event | category | flops | bytes accessed | tf_op | source)
XLA Modules:
  0.0 54.9 jit_solution(5192049930835182988)
XLA Ops:
  0.0 1.5 %collective-permute-start.6 = (bf16[16,8192]{1,0:T(8,128)(2,1)}, bf16[16,8192]{1,0:T(8,128)(2,1)S(1)}, u32[]{:S(2)}, u32[]{:S(2)}) collective-permute-start(bf16[16,8192]{1,0:T(8,128)(2,1)} %p0.3), channel_id=1, source_target_pairs={{0,1},{1,2},{2,3},{3,0},{4,5},{5,6},{6,7},{7,4},{8,9},{9,10},{10,1... | collective-permute-start | bytes 786440 | tf_op jit(solution)/shard_map/ppermute | solution.py:373
  1.5 2.7 %collective-permute-start.5 = (bf16[16,8192]{1,0:T(8,128)(2,1)}, bf16[16,8192]{1,0:T(8,128)(2,1)S(1)}, u32[]{:S(2)}, u32[]{:S(2)}) collective-permute-start(bf16[16,8192]{1,0:T(8,128)(2,1)} %p0.3), channel_id=1, source_target_pairs={{0,2},{1,3},{2,0},{3,1},{4,6},{5,7},{6,4},{7,5},{8,10},{9,11},{10,... | collective-permute-start | bytes 786440 | tf_op jit(solution)/shard_map/ppermute | solution.py:373
  4.2 1.4 %collective-permute-start.4 = (bf16[16,8192]{1,0:T(8,128)(2,1)}, bf16[16,8192]{1,0:T(8,128)(2,1)S(1)}, u32[]{:S(2)}, u32[]{:S(2)}) collective-permute-start(bf16[16,8192]{1,0:T(8,128)(2,1)} %p0.3), channel_id=1, source_target_pairs={{0,3},{1,0},{2,1},{3,2},{4,7},{5,4},{6,5},{7,6},{8,11},{9,8},{10,9... | collective-permute-start | bytes 786440 | tf_op jit(solution)/shard_map/ppermute | solution.py:373
  5.7 0.0 copy-start
  5.7 2.8 %upsweep.1 = (bf16[256,128]{1,0:T(8,128)(2,1)S(1)}, bf16[1,16,64]{2,1,0:T(8,128)(2,1)S(1)}) custom-call(bf16[16,8192]{1,0:T(8,128)(2,1)} %p0.3, bf16[32,64,256]{2,1,0:T(8,128)(2,1)} %basis_ref.1, bf16[31,64,128]{2,1,0:T(8,128)(2,1)} %bitcast.9), custom_call_target="tpu_custom_call" | custom-call | flops 8589934592 | bytes 1048576 | tf_op jit(solution)/shard_map/upsweep/pallas_call | solution.py:115
  8.5 0.1 collective-permute-start
  8.6 1.3 %collective-permute-done.second_ref = bf16[1,16,64]{2,1,0:T(8,128)(2,1)S(1)} collective-permute-done((bf16[1,16,64]{2,1,0:T(8,128)(2,1)S(1)}, bf16[1,16,64]{2,1,0:T(8,128)(2,1)S(1)}, u32[]{:S(2)}, u32[]{:S(2)}) %collective-permute-start) | collective-permute-done | bytes 2080 | tf_op jit(solution)/shard_map/ppermute | solution.py:378
  9.9 7.3 %collective-permute-start.1 = (bf16[2,16,64]{2,1,0:T(8,128)(2,1)S(1)}, bf16[2,16,64]{2,1,0:T(8,128)(2,1)S(1)}, u32[]{:S(2)}, u32[]{:S(2)}) collective-permute-start(bf16[2,16,64]{2,1,0:T(8,128)(2,1)S(1)} %append.5.first_ref.after_ref), channel_id=1, source_target_pairs={{0,248},{4,252},{8,0},{12,4},{16,8},{20,12},{24,16},{28,20},{32,24... | collective-permute-start | bytes 12296 | tf_op jit(solution)/shard_map/ppermute | solution.py:378
  17.3 1.4 %collective-permute-done.1.second_ref = bf16[2,16,64]{2,1,0:T(8,128)(2,1)S(1)} collective-permute-done((bf16[2,16,64]{2,1,0:T(8,128)(2,1)S(1)}, bf16[2,16,64]{2,1,0:T(8,128)(2,1)S(1)}, u32[]{:S(2)}, u32[]{:S(2)}) %collective-permute-start.1) | collective-permute-done | bytes 4128 | tf_op jit(solution)/shard_map/ppermute | solution.py:378
  18.6 5.8 %collective-permute-start.2 = (bf16[4,16,64]{2,1,0:T(8,128)(2,1)S(1)}, bf16[4,16,64]{2,1,0:T(8,128)(2,1)S(1)}, u32[]{:S(2)}, u32[]{:S(2)}) collective-permute-start(bf16[4,16,64]{2,1,0:T(8,128)(2,1)S(1)} %append.6.first_ref.after_ref), channel_id=1, source_target_pairs={{0,240},{4,244},{8,248},{12,252},{16,0},{20,4},{24,8},{28,12},{32,... | collective-permute-start | bytes 24584 | tf_op jit(solution)/shard_map/ppermute | solution.py:378
  24.5 0.0 collective-permute-done.6.p3
  24.5 0.0 collective-permute-done.5.p2
  24.5 0.0 collective-permute-done.4.p1
  24.5 0.0 copy-done
  24.5 0.0 slice-start.3
  24.6 4.8 %collective-permute-start.7 = (bf16[64,2176]{1,0:T(8,128)(2,1)S(1)}, bf16[64,2176]{1,0:T(8,128)(2,1)S(1)}, u32[]{:S(2)}, u32[]{:S(2)}) collective-permute-start(bf16[64,2176]{1,0:T(8,128)(2,1)S(1)} %get-tuple-element.15), channel_id=1, source_target_pairs={{0,4},{4,8},{8,12},{12,16},{16,20},{20,24},{24,28},{28,32},{32,36}... | collective-permute-start | bytes 835592 | tf_op jit(solution)/shard_map/ppermute | solution.py:383
  29.3 0.0 slice-start
  29.3 0.0 slice-start.1
  29.4 0.0 slice-start.2
  29.4 0.0 copy-start.6
  29.4 0.0 slice-start.4
  29.4 2.3 %collective-permute-start.8 = (bf16[64,2176]{1,0:T(8,128)(2,1)S(1)}, bf16[64,2176]{1,0:T(8,128)(2,1)S(1)}, u32[]{:S(2)}, u32[]{:S(2)}) collective-permute-start(bf16[64,2176]{1,0:T(8,128)(2,1)S(1)} %get-tuple-element.16), channel_id=1, source_target_pairs={{4,0},{8,4},{12,8},{16,12},{20,16},{24,20},{28,24},{32,28},{36,32}... | collective-permute-start | bytes 835592 | tf_op jit(solution)/shard_map/ppermute | solution.py:383
  31.7 0.0 collective-permute-done.2.second_ref
  31.7 0.1 collective-permute-start.3
  31.8 0.9 %collective-permute-done.7.left_ref = bf16[64,2176]{1,0:T(8,128)(2,1)S(1)} collective-permute-done((bf16[64,2176]{1,0:T(8,128)(2,1)S(1)}, bf16[64,2176]{1,0:T(8,128)(2,1)S(1)}, u32[]{:S(2)}, u32[]{:S(2)}) %collective-permute-start.7) | collective-permute-done | bytes 278560 | tf_op jit(solution)/shard_map/ppermute | solution.py:383
  32.7 3.1 %collective-permute-done.8.right_ref = bf16[64,2176]{1,0:T(8,128)(2,1)S(1)} collective-permute-done((bf16[64,2176]{1,0:T(8,128)(2,1)S(1)}, bf16[64,2176]{1,0:T(8,128)(2,1)S(1)}, u32[]{:S(2)}, u32[]{:S(2)}) %collective-permute-start.8) | collective-permute-done | bytes 278560 | tf_op jit(solution)/shard_map/ppermute | solution.py:383
  35.8 0.0 slice-done
  35.8 0.0 slice-done.1
  35.8 0.0 slice-done.2
  35.8 0.0 copy-done.6
  35.8 0.0 copy-start.5
  35.8 3.9 %near_field.1 = (bf16[256,384]{1,0:T(8,128)(2,1)S(1)}, bf16[256,384]{1,0:T(8,128)(2,1)S(1)}, bf16[256,384]{1,0:T(8,128)(2,1)S(1)}, bf16[256,384]{1,0:T(8,128)(2,1)S(1)}) custom-call(s32[3,32]{1,0:T(4,128)S(1)} %bitcast.12, bf16[16,8192]{1,0:T(8,128)(2,1)S(1)} %copy-done, bf16[16,8192]{1,0:T(8,128)(2,1)S(1)} %collective-permute-done.4.p1, ...), custom_call_target="tpu_custom_call" | custom-call | flops 6000000000 | bytes 4194304 | tf_op jit(solution)/shard_map/near_field/pallas_call | solution.py:209
  39.7 0.0 collective-permute-done.3.second_ref
  39.7 0.1 collective-permute-start.9
  39.8 0.7 %collective-permute-start.10 = (bf16[256,384]{1,0:T(8,128)(2,1)S(1)}, bf16[256,384]{1,0:T(8,128)(2,1)S(1)}, u32[]{:S(2)}, u32[]{:S(2)}) collective-permute-start(bf16[256,384]{1,0:T(8,128)(2,1)S(1)} %get-tuple-element.18), channel_id=1, source_target_pairs={{0,1},{1,2},{2,3},{3,0},{4,5},{5,6},{6,7},{7,4},{8,9},{9,10},{10,1... | collective-permute-start | bytes 589832 | tf_op jit(solution)/shard_map/ppermute | solution.py:373
  40.5 1.2 %collective-permute-start.11 = (bf16[256,384]{1,0:T(8,128)(2,1)S(1)}, bf16[256,384]{1,0:T(8,128)(2,1)S(1)}, u32[]{:S(2)}, u32[]{:S(2)}) collective-permute-start(bf16[256,384]{1,0:T(8,128)(2,1)S(1)} %get-tuple-element.19), channel_id=1, source_target_pairs={{0,2},{1,3},{2,0},{3,1},{4,6},{5,7},{6,4},{7,5},{8,10},{9,11},{10,... | collective-permute-start | bytes 589832 | tf_op jit(solution)/shard_map/ppermute | solution.py:373
  41.6 1.6 %collective-permute-start.12 = (bf16[256,384]{1,0:T(8,128)(2,1)S(1)}, bf16[256,384]{1,0:T(8,128)(2,1)S(1)}, u32[]{:S(2)}, u32[]{:S(2)}) collective-permute-start(bf16[256,384]{1,0:T(8,128)(2,1)S(1)} %get-tuple-element.20), channel_id=1, source_target_pairs={{0,3},{1,0},{2,1},{3,2},{4,7},{5,4},{6,5},{7,6},{8,11},{9,8},{10,9... | collective-permute-start | bytes 589832 | tf_op jit(solution)/shard_map/ppermute | solution.py:373
  43.2 0.0 slice-done.3
  43.2 0.0 slice-done.4
  43.2 0.0 copy-done.5
  43.2 0.0 copy-start.1
  43.3 0.0 copy-start.2
  43.3 0.0 copy-start.3
  43.3 0.0 copy-start.4
  43.3 2.6 %couple_leaves.1.after_ref.coupled_ref = f32[32,48,64]{2,1,0:T(8,128)S(1)} custom-call(s32[5,32]{1,0:T(8,128)S(1)} %bitcast.11, bf16[256,128]{1,0:T(8,128)(2,1)S(1)} %get-tuple-element.14.pairs_ref, bf16[64,2176]{1,0:T(8,128)(2,1)S(1)} %collective-permute-done.7.left_ref, bf16[64,2176]{1,0:T(8,128)(2,1)S(1)} %collective-permute-done.8.right_ref, ...), custom_call_target="tpu_custom_call" | custom-call | flops 3000000000 | bytes 4194304 | tf_op jit(solution)/shard_map/couple_leaves/pallas_call | solution.py:245
  45.9 0.3 collective-permute-done.9.first_ref
  46.2 0.0 copy-done.1
  46.2 0.0 copy-done.2
  46.2 0.0 copy-done.3
  46.2 0.0 copy-done.4
  46.2 3.3 %far_field.1.far_ref = f32[3,16,8192]{2,1,0:T(8,128)S(1)} custom-call(s32[1]{0:T(128)} %bitcast.1.where_ref, bf16[32,16,64]{2,1,0:T(8,128)(2,1)S(1)} %append.9.roots_ref, f32[32,48,64]{2,1,0:T(8,128)S(1)} %couple_leaves.1.after_ref.coupled_ref, bf16[3,1,64,192]{3,2,1,0:T(8,128)(2,1)S(1)} %copy-done.4, bf16[3,48,64,192]{3,2,1,0:T(8,128)(2,1)} %upper_hbm.1, ...), custom_call_target="tpu_custom_call" | custom-call | flops 3000000000 | bytes 4194304 | tf_op jit(solution)/shard_map/far_field/pallas_call | solution.py:329
  49.6 2.7 %collective-permute-done.10.n1 = bf16[256,384]{1,0:T(8,128)(2,1)S(1)} collective-permute-done((bf16[256,384]{1,0:T(8,128)(2,1)S(1)}, bf16[256,384]{1,0:T(8,128)(2,1)S(1)}, u32[]{:S(2)}, u32[]{:S(2)}) %collective-permute-start.10) | collective-permute-done | bytes 196640 | tf_op jit(solution)/shard_map/ppermute | solution.py:373
  52.3 0.0 collective-permute-done.11.n2
  52.3 1.2 %collective-permute-done.12.n3 = bf16[256,384]{1,0:T(8,128)(2,1)S(1)} collective-permute-done((bf16[256,384]{1,0:T(8,128)(2,1)S(1)}, bf16[256,384]{1,0:T(8,128)(2,1)S(1)}, u32[]{:S(2)}, u32[]{:S(2)}) %collective-permute-start.12) | collective-permute-done | bytes 196640 | tf_op jit(solution)/shard_map/ppermute | solution.py:373
  53.5 1.4 %join.1 = bf16[3,16,8192]{2,1,0:T(8,128)(2,1)} custom-call(s32[1]{0:T(128)} %bitcast.where_ref, f32[3,16,8192]{2,1,0:T(8,128)S(1)} %far_field.1.far_ref, bf16[256,384]{1,0:T(8,128)(2,1)S(1)} %get-tuple-element.17.after_ref.n0, bf16[256,384]{1,0:T(8,128)(2,1)S(1)} %collective-permute-done.10.n1, bf16[256,384]{1,0:T(8,128)(2,1)S(1)} %collective-permute-done.11.n2, ...), custom_call_target="tpu_custom_call" | custom-call | flops 1048576 | bytes 4194304 | tf_op jit(solution)/shard_map/join/pallas_call | solution.py:360
  (8 shorter events, 0.1 us)
Async XLA Ops:
  0.0 24.5 %collective-permute-start.6 = (bf16[16,8192]{1,0:T(8,128)(2,1)}, bf16[16,8192]{1,0:T(8,128)(2,1)S(1)}, u32[]{:S(2)}, u32[]{:S(2)}) collective-permute-start(bf16[16,8192]{1,0:T(8,128)(2,1)} %p0.3), channel_id=1, source_target_pairs={{0,1},{1,2},{2,3},{3,0},{4,5},{5,6},{6,7},{7,4},{8,9},{9,10},{10,1... | collective-permute-start | bytes 786440 | tf_op jit(solution)/shard_map/ppermute | solution.py:373
  1.5 23.0 %collective-permute-start.5 = (bf16[16,8192]{1,0:T(8,128)(2,1)}, bf16[16,8192]{1,0:T(8,128)(2,1)S(1)}, u32[]{:S(2)}, u32[]{:S(2)}) collective-permute-start(bf16[16,8192]{1,0:T(8,128)(2,1)} %p0.3), channel_id=1, source_target_pairs={{0,2},{1,3},{2,0},{3,1},{4,6},{5,7},{6,4},{7,5},{8,10},{9,11},{10,... | collective-permute-start | bytes 786440 | tf_op jit(solution)/shard_map/ppermute | solution.py:373
  4.2 20.3 %collective-permute-start.4 = (bf16[16,8192]{1,0:T(8,128)(2,1)}, bf16[16,8192]{1,0:T(8,128)(2,1)S(1)}, u32[]{:S(2)}, u32[]{:S(2)}) collective-permute-start(bf16[16,8192]{1,0:T(8,128)(2,1)} %p0.3), channel_id=1, source_target_pairs={{0,3},{1,0},{2,1},{3,2},{4,7},{5,4},{6,5},{7,6},{8,11},{9,8},{10,9... | collective-permute-start | bytes 786440 | tf_op jit(solution)/shard_map/ppermute | solution.py:373
  5.7 18.8 %copy-start = (bf16[16,8192]{1,0:T(8,128)(2,1)S(1)}, bf16[16,8192]{1,0:T(8,128)(2,1)}, u32[]{:S(2)}) copy-start(bf16[16,8192]{1,0:T(8,128)(2,1)} %p0.3) | copy-start | bytes 786436
  8.5 1.4 %collective-permute-start = (bf16[1,16,64]{2,1,0:T(8,128)(2,1)S(1)}, bf16[1,16,64]{2,1,0:T(8,128)(2,1)S(1)}, u32[]{:S(2)}, u32[]{:S(2)}) collective-permute-start(bf16[1,16,64]{2,1,0:T(8,128)(2,1)S(1)} %get-tuple-element.13.first_ref.after_ref), channel_id=1, source_target_pairs={{0,252},{4,0},{8,4},{12,8},{16,12},{20,16},{24,20},{28,24},{32,28}... | collective-permute-start | bytes 6152 | tf_op jit(solution)/shard_map/ppermute | solution.py:378
  9.9 8.7 %collective-permute-start.1 = (bf16[2,16,64]{2,1,0:T(8,128)(2,1)S(1)}, bf16[2,16,64]{2,1,0:T(8,128)(2,1)S(1)}, u32[]{:S(2)}, u32[]{:S(2)}) collective-permute-start(bf16[2,16,64]{2,1,0:T(8,128)(2,1)S(1)} %append.5.first_ref.after_ref), channel_id=1, source_target_pairs={{0,248},{4,252},{8,0},{12,4},{16,8},{20,12},{24,16},{28,20},{32,24... | collective-permute-start | bytes 12296 | tf_op jit(solution)/shard_map/ppermute | solution.py:378
  18.6 13.1 %collective-permute-start.2 = (bf16[4,16,64]{2,1,0:T(8,128)(2,1)S(1)}, bf16[4,16,64]{2,1,0:T(8,128)(2,1)S(1)}, u32[]{:S(2)}, u32[]{:S(2)}) collective-permute-start(bf16[4,16,64]{2,1,0:T(8,128)(2,1)S(1)} %append.6.first_ref.after_ref), channel_id=1, source_target_pairs={{0,240},{4,244},{8,248},{12,252},{16,0},{20,4},{24,8},{28,12},{32,... | collective-permute-start | bytes 24584 | tf_op jit(solution)/shard_map/ppermute | solution.py:378
  24.5 18.7 %slice-start.3 = ((s8[4718592]{0:T(1024)(128)(4,1)}), s8[4194304]{0:T(1024)(128)(4,1)S(1)}, s32[]{:S(2)}) async-start(s8[4718592]{0:T(1024)(128)(4,1)} %bitcast.7), calls=%async_computation.3 | async-start | bytes 8388608
  24.6 8.1 %collective-permute-start.7 = (bf16[64,2176]{1,0:T(8,128)(2,1)S(1)}, bf16[64,2176]{1,0:T(8,128)(2,1)S(1)}, u32[]{:S(2)}, u32[]{:S(2)}) collective-permute-start(bf16[64,2176]{1,0:T(8,128)(2,1)S(1)} %get-tuple-element.15), channel_id=1, source_target_pairs={{0,4},{4,8},{8,12},{12,16},{16,20},{20,24},{24,28},{28,32},{32,36}... | collective-permute-start | bytes 835592 | tf_op jit(solution)/shard_map/ppermute | solution.py:383
  29.3 6.4 %slice-start = ((s8[9437184]{0:T(1024)(128)(4,1)}), s8[4194304]{0:T(1024)(128)(4,1)S(1)}, s32[]{:S(2)}) async-start(s8[9437184]{0:T(1024)(128)(4,1)} %bitcast.5), calls=%async_computation | async-start | bytes 8388608
  29.3 6.4 %slice-start.1 = ((s8[9437184]{0:T(1024)(128)(4,1)}), s8[4194304]{0:T(1024)(128)(4,1)S(1)}, s32[]{:S(2)}) async-start(s8[9437184]{0:T(1024)(128)(4,1)} %bitcast.5), calls=%async_computation.1 | async-start | bytes 8388608
  29.4 6.4 %slice-start.2 = ((s8[9437184]{0:T(1024)(128)(4,1)}), s8[1048576]{0:T(1024)(128)(4,1)S(1)}, s32[]{:S(2)}) async-start(s8[9437184]{0:T(1024)(128)(4,1)} %bitcast.5), calls=%async_computation.2 | async-start | bytes 2097152
  29.4 6.4 %copy-start.6 = (s32[32,3]{0,1:T(4,128)S(1)}, s32[32,3]{0,1:T(4,128)}, u32[]{:S(2)}) copy-start(s32[32,3]{0,1:T(4,128)} %param.18) | copy-start | bytes 1156
  29.4 13.9 %slice-start.4 = ((s8[4718592]{0:T(1024)(128)(4,1)}), s8[524288]{0:T(1024)(128)(4,1)S(1)}, s32[]{:S(2)}) async-start(s8[4718592]{0:T(1024)(128)(4,1)} %bitcast.7), calls=%async_computation.4 | async-start | bytes 1048576
  29.4 6.4 %collective-permute-start.8 = (bf16[64,2176]{1,0:T(8,128)(2,1)S(1)}, bf16[64,2176]{1,0:T(8,128)(2,1)S(1)}, u32[]{:S(2)}, u32[]{:S(2)}) collective-permute-start(bf16[64,2176]{1,0:T(8,128)(2,1)S(1)} %get-tuple-element.16), channel_id=1, source_target_pairs={{4,0},{8,4},{12,8},{16,12},{20,16},{24,20},{28,24},{32,28},{36,32}... | collective-permute-start | bytes 835592 | tf_op jit(solution)/shard_map/ppermute | solution.py:383
  31.7 7.9 %collective-permute-start.3 = (bf16[8,16,64]{2,1,0:T(8,128)(2,1)S(1)}, bf16[8,16,64]{2,1,0:T(8,128)(2,1)S(1)}, u32[]{:S(2)}, u32[]{:S(2)}) collective-permute-start(bf16[8,16,64]{2,1,0:T(8,128)(2,1)S(1)} %append.7.first_ref), channel_id=1, source_target_pairs={{0,224},{4,228},{8,232},{12,236},{16,240},{20,244},{24,248},{28,25... | collective-permute-start | bytes 49160 | tf_op jit(solution)/shard_map/ppermute | solution.py:378
  35.8 7.5 %copy-start.5 = (s32[32,5]{0,1:T(8,128)S(1)}, s32[32,5]{0,1:T(8,128)}, u32[]{:S(2)}) copy-start(s32[32,5]{0,1:T(8,128)} %param.19) | copy-start | bytes 1924
  39.7 6.5 %collective-permute-start.9 = (bf16[16,16,64]{2,1,0:T(8,128)(2,1)S(1)}, bf16[16,16,64]{2,1,0:T(8,128)(2,1)S(1)}, u32[]{:S(2)}, u32[]{:S(2)}) collective-permute-start(bf16[16,16,64]{2,1,0:T(8,128)(2,1)S(1)} %append.8.second_ref), channel_id=1, source_target_pairs={{0,64},{4,68},{8,72},{12,76},{16,80},{20,84},{24,88},{28,92},{32,9... | collective-permute-start | bytes 98312 | tf_op jit(solution)/shard_map/ppermute | solution.py:378
  39.8 12.5 %collective-permute-start.10 = (bf16[256,384]{1,0:T(8,128)(2,1)S(1)}, bf16[256,384]{1,0:T(8,128)(2,1)S(1)}, u32[]{:S(2)}, u32[]{:S(2)}) collective-permute-start(bf16[256,384]{1,0:T(8,128)(2,1)S(1)} %get-tuple-element.18), channel_id=1, source_target_pairs={{0,1},{1,2},{2,3},{3,0},{4,5},{5,6},{6,7},{7,4},{8,9},{9,10},{10,1... | collective-permute-start | bytes 589832 | tf_op jit(solution)/shard_map/ppermute | solution.py:373
  40.5 11.8 %collective-permute-start.11 = (bf16[256,384]{1,0:T(8,128)(2,1)S(1)}, bf16[256,384]{1,0:T(8,128)(2,1)S(1)}, u32[]{:S(2)}, u32[]{:S(2)}) collective-permute-start(bf16[256,384]{1,0:T(8,128)(2,1)S(1)} %get-tuple-element.19), channel_id=1, source_target_pairs={{0,2},{1,3},{2,0},{3,1},{4,6},{5,7},{6,4},{7,5},{8,10},{9,11},{10,... | collective-permute-start | bytes 589832 | tf_op jit(solution)/shard_map/ppermute | solution.py:373
  41.6 11.9 %collective-permute-start.12 = (bf16[256,384]{1,0:T(8,128)(2,1)S(1)}, bf16[256,384]{1,0:T(8,128)(2,1)S(1)}, u32[]{:S(2)}, u32[]{:S(2)}) collective-permute-start(bf16[256,384]{1,0:T(8,128)(2,1)S(1)} %get-tuple-element.20), channel_id=1, source_target_pairs={{0,3},{1,0},{2,1},{3,2},{4,7},{5,4},{6,5},{7,6},{8,11},{9,8},{10,9... | collective-permute-start | bytes 589832 | tf_op jit(solution)/shard_map/ppermute | solution.py:373
  43.2 2.9 %copy-start.1 = (bf16[32,64,256]{2,1,0:T(8,128)(2,1)S(1)}, bf16[32,64,256]{2,1,0:T(8,128)(2,1)}, u32[]{:S(2)}) copy-start(bf16[32,64,256]{2,1,0:T(8,128)(2,1)} %basis_ref.1) | copy-start | bytes 3145732
  43.3 2.9 %copy-start.2 = (bf16[48,64,128]{2,1,0:T(8,128)(2,1)S(1)}, bf16[48,64,128]{2,1,0:T(8,128)(2,1)}, u32[]{:S(2)}) copy-start(bf16[48,64,128]{2,1,0:T(8,128)(2,1)} %top_ref.1) | copy-start | bytes 2359300
  43.3 2.9 %copy-start.3 = (bf16[1,31,64,128]{3,2,1,0:T(8,128)(2,1)S(1)}, bf16[1,31,64,128]{3,2,1,0:T(8,128)(2,1)}, u32[]{:S(2)}) copy-start(bf16[1,31,64,128]{3,2,1,0:T(8,128)(2,1)} %param.12) | copy-start | bytes 1523716
  43.3 2.9 %copy-start.4 = (bf16[3,1,64,192]{3,2,1,0:T(8,128)(2,1)S(1)}, bf16[3,1,64,192]{3,2,1,0:T(8,128)(2,1)}, u32[]{:S(2)}) copy-start(bf16[3,1,64,192]{3,2,1,0:T(8,128)(2,1)} %root_ref.1) | copy-start | bytes 221188
